TPU v7x, 256 devices: a whole 4x4x8 slice. The times are simulated.
256 devices in a mesh: dp: 16 (over y, x), expert: 16 (over z, core).
Axes of the slice: x: 4, y: 4, z: 8, core: 2. Of those that a mesh axis runs over, the one named last changes fastest.
Arguments:
- tokens: bfloat16 [32768, 2048], P(('dp', 'expert')), may hold values from -6 to 6
- expert_ids: int32 [32768, 8], P(('dp', 'expert')), may hold values from 0 to 127, as said below
- gate_weights: float32 [32768, 8], P(('dp', 'expert')), may hold values from 0.1 to 1
- w_gate: bfloat16 [16, 2048, 768], P('expert'), may hold values from -0.125 to 0.125
- w_up: bfloat16 [16, 2048, 768], P('expert'), may hold values from -0.125 to 0.125
- w_down: bfloat16 [16, 768, 2048], P('expert'), may hold values from -0.21875 to 0.21875
- cotangent: bfloat16 [32768, 2048], P(('dp', 'expert')), may hold values from -6 to 6
Outputs:
- combined: bfloat16 [32768, 2048], P(('dp', 'expert'))
- grad_tokens: bfloat16 [32768, 2048], P(('dp', 'expert'))
- grad_gate: float32 [16, 2048, 768], P('expert', 'dp')
- grad_up: float32 [16, 2048, 768], P('expert', 'dp')
- grad_down: float32 [16, 768, 2048], P('expert', None, 'dp')
Inputs may be any that keep to these rules, and one draw needn't show every extreme that they name: `expert_ids`: each row names 8 different experts; its k-th entry (k from 0) lies in k * 16 to (k + 1) * 16 - 1. In the rows of one device no expert is named more than 24 times. In the rows of each run of 16 devices along expert (one index of dp), one expert below 16 is named exactly 24 times by every device.
All inputs are finite; a program needn't handle non-finite values.
Results may differ from a plain program's by a relative error of at most 0.0057.
Values may be sent and summed in bfloat16 or wider, within the bound.
A program may use at most 128 MiB of HBM per device.

v0:
```python
import jax
import jax.numpy as jnp
from jax import lax
from jax.sharding import PartitionSpec as P

CAP = 24


def local(tokens, expert_ids, gate_weights, w_gate, w_up, w_down, cotangent):
    rows_here = tokens.shape[0]
    model_width = tokens.shape[1]
    groups = lax.axis_size("expert")
    per_dev = w_gate.shape[0]
    live_total = groups * per_dev
    capacity = CAP
    chosen = expert_ids[:, :, None] == jnp.arange(live_total, dtype=jnp.int32)[None, None, :]
    hit_table = jnp.sum(chosen.astype(jnp.float32), axis=1)
    scales = jnp.sum(jnp.where(chosen, gate_weights[:, :, None], jnp.float32(0.0)), axis=1)
    row_index = jnp.arange(rows_here, dtype=jnp.int32)
    earlier_mask = (row_index[None, :] < row_index[:, None]).astype(jnp.float32)
    before = jnp.dot(earlier_mask, hit_table, precision=lax.Precision.HIGHEST)
    slot_index = jnp.arange(capacity, dtype=jnp.float32)
    placement = hit_table.T[:, None, :] * (
        before.T[:, None, :] == slot_index[None, :, None]
    ).astype(jnp.float32)
    placement = placement.reshape(groups, per_dev, capacity, rows_here).transpose(1, 0, 2, 3)
    scale_grid = scales.T.reshape(groups, per_dev, 1, rows_here).transpose(1, 0, 2, 3)
    weighted = placement * scale_grid
    place_bf16 = placement.astype(jnp.bfloat16)
    outgoing = jnp.einsum(
        "enct,td->encd", place_bf16, tokens, preferred_element_type=jnp.float32
    ).astype(jnp.bfloat16)
    incoming = lax.all_to_all(outgoing, "expert", split_axis=1, concat_axis=1, tiled=True).reshape(
        per_dev, groups * capacity, model_width
    )
    gate_pre = jnp.einsum("erd,edf->erf", incoming, w_gate, preferred_element_type=jnp.float32)
    up_pre = jnp.einsum("erd,edf->erf", incoming, w_up, preferred_element_type=jnp.float32)
    sigmoid_gate = jax.nn.sigmoid(gate_pre)
    activated = gate_pre * sigmoid_gate
    hidden = (activated * up_pre).astype(jnp.bfloat16)
    result = jnp.einsum("erf,efd->erd", hidden, w_down, preferred_element_type=jnp.float32).astype(
        jnp.bfloat16
    )
    result = result.reshape(per_dev, groups, capacity, model_width)
    returned = lax.all_to_all(result, "expert", split_axis=1, concat_axis=1, tiled=True)
    combined = jnp.einsum(
        "enct,encd->td", weighted, returned.astype(jnp.float32), precision=lax.Precision.HIGHEST
    ).astype(jnp.bfloat16)
    scaled_grad = jnp.einsum(
        "enct,td->encd", weighted, cotangent.astype(jnp.float32), precision=lax.Precision.HIGHEST
    ).astype(jnp.bfloat16)
    grad_rows = lax.all_to_all(
        scaled_grad, "expert", split_axis=1, concat_axis=1, tiled=True
    ).reshape(per_dev, groups * capacity, model_width)
    grad_hidden = jnp.einsum("erd,efd->erf", grad_rows, w_down, preferred_element_type=jnp.float32)
    grad_gate_pre = (
        grad_hidden * up_pre * sigmoid_gate * (1.0 + gate_pre * (1.0 - sigmoid_gate))
    ).astype(jnp.bfloat16)
    grad_up_pre = (grad_hidden * activated).astype(jnp.bfloat16)
    grad_input = (
        jnp.einsum("erf,edf->erd", grad_gate_pre, w_gate, preferred_element_type=jnp.float32)
        + jnp.einsum("erf,edf->erd", grad_up_pre, w_up, preferred_element_type=jnp.float32)
    ).astype(jnp.bfloat16)
    grad_input = grad_input.reshape(per_dev, groups, capacity, model_width)
    local_gate = jnp.einsum(
        "erd,erf->edf", incoming, grad_gate_pre, preferred_element_type=jnp.float32
    )
    local_up = jnp.einsum("erd,erf->edf", incoming, grad_up_pre, preferred_element_type=jnp.float32)
    local_down = jnp.einsum("erf,erd->efd", hidden, grad_rows, preferred_element_type=jnp.float32)
    grad_gate, grad_up, grad_down = (
        lax.psum_scatter(local_gate, "dp", scatter_dimension=1, tiled=True),
        lax.psum_scatter(local_up, "dp", scatter_dimension=1, tiled=True),
        lax.psum_scatter(local_down, "dp", scatter_dimension=2, tiled=True),
    )
    grad_back = lax.all_to_all(grad_input, "expert", split_axis=1, concat_axis=1, tiled=True)
    grad_tokens = jnp.einsum(
        "enct,encd->td", place_bf16, grad_back, preferred_element_type=jnp.float32
    ).astype(jnp.bfloat16)
    return (combined, grad_tokens, grad_gate, grad_up, grad_down)


def solution(mesh):
    in_specs = (
        P(("dp", "expert"), None),
        P(("dp", "expert"), None),
        P(("dp", "expert"), None),
        P("expert", None, None),
        P("expert", None, None),
        P("expert", None, None),
        P(("dp", "expert"), None),
    )
    out_specs = (
        P(("dp", "expert"), None),
        P(("dp", "expert"), None),
        P("expert", "dp", None),
        P("expert", "dp", None),
        P("expert", None, "dp"),
    )
    return jax.shard_map(local, mesh=mesh, in_specs=in_specs, out_specs=out_specs, check_vma=False)
```

profile of v0, /device:TPU:1, one launch (start us, length us, event | category | flops | bytes accessed | tf_op | source)
XLA Modules:
  0.0 387.7 jit_solution(11149249703975599784)
XLA Ops:
  7.2 0.0 copy-start
  7.2 0.9 select_reduce_fusion
  8.1 0.1 fusion.40
  8.2 2.8 fusion.17
  11.0 10.0 %all-to-all-start = ((bf16[1,16,24,2048]{3,2,0,1:T(8,128)(2,1)}), bf16[1,16,24,2048]{3,2,0,1:T(8,128)(2,1)}, u32[]{:S(2)}, u32[]{:S(2)}) async-start(bf16[1,16,24,2048]{3,2,0,1:T(8,128)(2,1)} %fusion.17), calls=%async_computation | async-start | bytes 3145728 | tf_op jit(solution)/shard_map/all_to_all | solution.py:33
  21.0 3.6 fusion.18
  24.5 35.0 %all-to-all-done = bf16[1,16,24,2048]{3,2,0,1:T(8,128)(2,1)} async-done(((bf16[1,16,24,2048]{3,2,0,1:T(8,128)(2,1)}), bf16[1,16,24,2048]{3,2,0,1:T(8,128)(2,1)}, u32[]{:S(2)}, u32[]{:S(2)}) %all-to-all-start) | async-done | bytes 1572896 | tf_op jit(solution)/shard_map/all_to_all | solution.py:33
  59.5 4.3 %all-to-all-start.2 = ((bf16[1,16,24,2048]{3,2,0,1:T(8,128)(2,1)}), bf16[1,16,24,2048]{3,2,0,1:T(8,128)(2,1)}, u32[]{:S(2)}, u32[]{:S(2)}) async-start(bf16[1,16,24,2048]{3,2,0,1:T(8,128)(2,1)} %fusion.18), calls=%async_computation.2 | async-start | bytes 3145728 | tf_op jit(solution)/shard_map/all_to_all | solution.py:52
  63.8 0.0 reduce-scatter.4.cloned.1.call-start
  63.9 4.8 %fusion.6 = f32[384,768]{1,0:T(8,128)} fusion(bf16[384,2048]{1,0:T(8,128)(2,1)} %bitcast.5, bf16[1,2048,768]{2,1,0:T(8,128)(2,1)} %param.11), kind=kOutput, calls=%fused_computation.9 | convolution fusion | flops 1207959552 | bytes 5898240 | tf_op jit(solution)/shard_map/erd,edf->erf/dot_general | solution.py:37
  68.7 33.7 %all-to-all-done.2 = bf16[1,16,24,2048]{3,2,0,1:T(8,128)(2,1)} async-done(((bf16[1,16,24,2048]{3,2,0,1:T(8,128)(2,1)}), bf16[1,16,24,2048]{3,2,0,1:T(8,128)(2,1)}, u32[]{:S(2)}, u32[]{:S(2)}) %all-to-all-start.2) | async-done | bytes 1572896 | tf_op jit(solution)/shard_map/all_to_all | solution.py:52
  102.3 0.0 copy-start.3
  102.3 3.9 %fusion = f32[384,768]{1,0:T(8,128)S(1)} fusion(bf16[384,2048]{1,0:T(8,128)(2,1)} %bitcast.16, bf16[1,768,2048]{2,1,0:T(8,128)(2,1)} %param.12), kind=kOutput, calls=%fused_computation.3 | convolution fusion | flops 1207959552 | bytes 5898240 | tf_op jit(solution)/shard_map/erd,efd->erf/dot_general | solution.py:55
  106.2 0.0 copy-done
  106.2 0.0 copy-done.3
  106.2 4.2 %multiply_convert_fusion.1 = (bf16[384,768]{1,0:T(8,128)(2,1)S(1)}, bf16[384,768]{1,0:T(8,128)(2,1)}, bf16[384,768]{1,0:T(8,128)(2,1)}) fusion(f32[384,768]{1,0:T(8,128)S(1)} %fusion, f32[384,768]{1,0:T(8,128)S(1)} %copy-done.3, bf16[384,2048]{1,0:T(8,128)(2,1)} %bitcast.5, bf16[1,2048,768]{2,1,0:T(8,128)(2,1)S(1)} %copy-done), kind=kOutput, calls=%fused_computation.28 | convolution fusion | flops 1212383232 | bytes 8847360 | tf_op jit(solution)/shard_map/erd,edf->erf/dot_general | solution.py:36
  110.5 0.0 copy-start.1
  110.5 0.8 copy-done.1
  111.3 5.9 %convolution_bitcast_fusion.2 = f32[1,2048,768]{2,1,0:T(8,128)} fusion(bf16[384,2048]{1,0:T(8,128)(2,1)} %bitcast.5, bf16[384,768]{1,0:T(8,128)(2,1)S(1)} %get-tuple-element.7), kind=kOutput, calls=%fused_computation.2 | convolution fusion | flops 1207959552 | bytes 8454144 | tf_op jit(solution)/shard_map/erd,erf->edf/dot_general | solution.py:65
  117.2 0.0 reduce-scatter.4.cloned.1.call-update
  117.2 0.0 reduce-scatter.6.cloned.1.call-start
  117.3 6.0 %convolution_bitcast_fusion.1 = f32[1,2048,768]{2,1,0:T(8,128)} fusion(bf16[384,2048]{1,0:T(8,128)(2,1)} %bitcast.5, bf16[384,768]{1,0:T(8,128)(2,1)} %get-tuple-element.8), kind=kOutput, calls=%fused_computation.1 | convolution fusion | flops 1207959552 | bytes 8454144 | tf_op jit(solution)/shard_map/erd,erf->edf/dot_general | solution.py:68
  123.3 0.0 reduce-scatter.6.cloned.1.call-update
  123.3 0.2 reduce-scatter.8.cloned.1.call-start
  123.5 6.0 %convolution_bitcast_fusion = f32[1,768,2048]{2,1,0:T(8,128)} fusion(bf16[384,768]{1,0:T(8,128)(2,1)} %get-tuple-element.9, bf16[384,2048]{1,0:T(8,128)(2,1)} %bitcast.16), kind=kOutput, calls=%fused_computation | convolution fusion | flops 1207959552 | bytes 8454144 | tf_op jit(solution)/shard_map/erf,erd->efd/dot_general | solution.py:69
  129.6 0.0 reduce-scatter.8.cloned.1.call-update
  129.6 0.0 copy-start.2
  129.6 3.5 fusion.4
  133.2 0.0 copy-done.2
  133.2 2.6 add_convert_fusion
  135.8 4.5 %all-to-all-start.3 = ((bf16[1,16,24,2048]{3,2,0,1:T(8,128)(2,1)}), bf16[1,16,24,2048]{3,2,0,1:T(8,128)(2,1)}, u32[]{:S(2)}, u32[]{:S(2)}) async-start(bf16[1,16,24,2048]{3,2,0,1:T(8,128)(2,1)} %bitcast.79), calls=%async_computation.3 | async-start | bytes 3145728 | tf_op jit(solution)/shard_map/all_to_all | solution.py:75
  140.3 4.7 %fusion.14 = bf16[384,2048]{1,0:T(8,128)(2,1)} fusion(bf16[384,768]{1,0:T(8,128)(2,1)} %get-tuple-element.9, bf16[1,768,2048]{2,1,0:T(8,128)(2,1)} %param.12), kind=kOutput, calls=%fused_computation.16 | convolution fusion | flops 1208745984 | bytes 5308416 | tf_op jit(solution)/shard_map/erf,efd->erd/dot_general | solution.py:41
  145.0 33.9 %all-to-all-done.3 = bf16[1,16,24,2048]{3,2,0,1:T(8,128)(2,1)} async-done(((bf16[1,16,24,2048]{3,2,0,1:T(8,128)(2,1)}), bf16[1,16,24,2048]{3,2,0,1:T(8,128)(2,1)}, u32[]{:S(2)}, u32[]{:S(2)}) %all-to-all-start.3) | async-done | bytes 1572896 | tf_op jit(solution)/shard_map/all_to_all | solution.py:75
  178.9 4.3 %all-to-all-start.1 = ((bf16[1,16,24,2048]{3,2,0,1:T(8,128)(2,1)}), bf16[1,16,24,2048]{3,2,0,1:T(8,128)(2,1)}, u32[]{:S(2)}, u32[]{:S(2)}) async-start(bf16[1,16,24,2048]{3,2,0,1:T(8,128)(2,1)} %bitcast.78), calls=%async_computation.1 | async-start | bytes 3145728 | tf_op jit(solution)/shard_map/all_to_all | solution.py:45
  183.2 2.7 fusion.20
  185.9 35.8 %all-to-all-done.1 = bf16[1,16,24,2048]{3,2,0,1:T(8,128)(2,1)} async-done(((bf16[1,16,24,2048]{3,2,0,1:T(8,128)(2,1)}), bf16[1,16,24,2048]{3,2,0,1:T(8,128)(2,1)}, u32[]{:S(2)}, u32[]{:S(2)}) %all-to-all-start.1) | async-done | bytes 1572896 | tf_op jit(solution)/shard_map/all_to_all | solution.py:45
  221.7 3.3 fusion.19
  224.9 0.0 reduce-scatter.4.cloned.1.call-done
  224.9 66.1 %reduce-scatter.6.cloned.1.call-done = f32[1,128,768]{2,1,0:T(8,128)} async-done(((f32[1,2048,768]{2,1,0:T(8,128)}), f32[1,128,768]{2,1,0:T(8,128)}) %reduce-scatter.6.cloned.1.call-update) | async-done | bytes 393232 | tf_op jit(solution)/shard_map/reduce_scatter | solution.py:72
  291.0 90.2 %reduce-scatter.8.cloned.1.call-done = f32[1,768,128]{2,1,0:T(8,128)} async-done(((f32[1,768,2048]{2,1,0:T(8,128)}), f32[1,768,128]{2,1,0:T(8,128)}) %reduce-scatter.8.cloned.1.call-update) | async-done | bytes 393232 | tf_op jit(solution)/shard_map/reduce_scatter | solution.py:73
Async XLA Ops:
  7.2 99.0 %copy-start = (bf16[1,2048,768]{2,1,0:T(8,128)(2,1)S(1)}, bf16[1,2048,768]{2,1,0:T(8,128)(2,1)}, u32[]{:S(2)}) copy-start(bf16[1,2048,768]{2,1,0:T(8,128)(2,1)} %param.10) | copy-start | bytes 9437188
  11.0 48.5 %all-to-all-start = ((bf16[1,16,24,2048]{3,2,0,1:T(8,128)(2,1)}), bf16[1,16,24,2048]{3,2,0,1:T(8,128)(2,1)}, u32[]{:S(2)}, u32[]{:S(2)}) async-start(bf16[1,16,24,2048]{3,2,0,1:T(8,128)(2,1)} %fusion.17), calls=%async_computation | async-start | bytes 3145728 | tf_op jit(solution)/shard_map/all_to_all | solution.py:33
  59.5 42.8 %all-to-all-start.2 = ((bf16[1,16,24,2048]{3,2,0,1:T(8,128)(2,1)}), bf16[1,16,24,2048]{3,2,0,1:T(8,128)(2,1)}, u32[]{:S(2)}, u32[]{:S(2)}) async-start(bf16[1,16,24,2048]{3,2,0,1:T(8,128)(2,1)} %fusion.18), calls=%async_computation.2 | async-start | bytes 3145728 | tf_op jit(solution)/shard_map/all_to_all | solution.py:52
  63.8 161.1 %reduce-scatter.4.cloned.1.call-start = ((), (), s32[]{:S(2)}) async-start(), calls=%async_computation.7 | async-start | bytes 6684672 | tf_op jit(solution)/shard_map/reduce_scatter | solution.py:71
  102.3 3.9 %copy-start.3 = (f32[384,768]{1,0:T(8,128)S(1)}, f32[384,768]{1,0:T(8,128)}, u32[]{:S(2)}) copy-start(f32[384,768]{1,0:T(8,128)} %fusion.6) | copy-start | bytes 3538948
  110.5 0.8 copy-start.1
  117.2 173.8 %reduce-scatter.6.cloned.1.call-start = ((), (), s32[]{:S(2)}) async-start(), calls=%async_computation.8 | async-start | bytes 6684672 | tf_op jit(solution)/shard_map/reduce_scatter | solution.py:72
  123.3 257.9 %reduce-scatter.8.cloned.1.call-start = ((), (), s32[]{:S(2)}) async-start(), calls=%async_computation.9 | async-start | bytes 6684672 | tf_op jit(solution)/shard_map/reduce_scatter | solution.py:73
  129.6 3.6 copy-start.2
  135.8 43.1 %all-to-all-start.3 = ((bf16[1,16,24,2048]{3,2,0,1:T(8,128)(2,1)}), bf16[1,16,24,2048]{3,2,0,1:T(8,128)(2,1)}, u32[]{:S(2)}, u32[]{:S(2)}) async-start(bf16[1,16,24,2048]{3,2,0,1:T(8,128)(2,1)} %bitcast.79), calls=%async_computation.3 | async-start | bytes 3145728 | tf_op jit(solution)/shard_map/all_to_all | solution.py:75
  178.9 42.8 %all-to-all-start.1 = ((bf16[1,16,24,2048]{3,2,0,1:T(8,128)(2,1)}), bf16[1,16,24,2048]{3,2,0,1:T(8,128)(2,1)}, u32[]{:S(2)}, u32[]{:S(2)}) async-start(bf16[1,16,24,2048]{3,2,0,1:T(8,128)(2,1)} %bitcast.78), calls=%async_computation.1 | async-start | bytes 3145728 | tf_op jit(solution)/shard_map/all_to_all | solution.py:45
Sparse Core Ops, SparseCore 0:
  117.4 83.4 reduce-scatter.3
  205.2 85.8 reduce-scatter.5
  295.3 85.8 reduce-scatter.7
where the time goes:
time: 388 us
  waiting for transfers between devices  295 us (76%)
  matrix products  54.2 us (14%)
  starting transfers between devices  23.4 us (6%)
  between operations  13.8 us (4%)
    reduce_scatter x1, waiting for transfers between devices, local(): lax.psum_scatter(local_down, 'dp', scatter_dimension=2, tiled=True)  90.2 us
    reduce_scatter x1, waiting for transfers between devices, local(): lax.psum_scatter(local_up, 'dp', scatter_dimension=1, tiled=True)  66.1 us
    all_to_all x1, waiting for transfers between devices, local(): lax.all_to_all(result, 'expert', split_axis=1, concat_axis=1, tiled=True)  35.8 us
    all_to_all x1, waiting for transfers between devices, local(): lax.all_to_all(outgoing, 'expert', split_axis=1, concat_axis=1, tiled=True)  35 us
    all_to_all x1, waiting for transfers between devices, local(): lax.all_to_all(grad_input, 'expert', split_axis=1, concat_axis=1, tiled=T...  33.9 us
    all_to_all x1, waiting for transfers between devices, local(): lax.all_to_all(scaled_grad, 'expert', split_axis=1, concat_axis=1, tiled=...  33.7 us
    all_to_all x1, starting transfers between devices, local(): lax.all_to_all(outgoing, 'expert', split_axis=1, concat_axis=1, tiled=True)  9.98 us
  transfers between devices with their start and end apart: 7, of which 6 were waited for; matrix products, arithmetic and copies ran while one was open for 10% of the time, Pallas kernels for 0%

commit v1 on v0

--- a/solution.py
+++ b/solution.py
@@ -13,9 +13,9 @@
     per_dev = w_gate.shape[0]
     live_total = groups * per_dev
     capacity = CAP
-    chosen = expert_ids[:, :, None] == jnp.arange(live_total, dtype=jnp.int32)[None, None, :]
-    hit_table = jnp.sum(chosen.astype(jnp.float32), axis=1)
-    scales = jnp.sum(jnp.where(chosen, gate_weights[:, :, None], jnp.float32(0.0)), axis=1)
+    chosen = expert_ids[:, :1] == jnp.arange(live_total, dtype=jnp.int32)[None, :]
+    hit_table = chosen.astype(jnp.float32)
+    weight = gate_weights[:, :1]
     row_index = jnp.arange(rows_here, dtype=jnp.int32)
     earlier_mask = (row_index[None, :] < row_index[:, None]).astype(jnp.float32)
     before = jnp.dot(earlier_mask, hit_table, precision=lax.Precision.HIGHEST)
@@ -24,8 +24,6 @@
         before.T[:, None, :] == slot_index[None, :, None]
     ).astype(jnp.float32)
     placement = placement.reshape(groups, per_dev, capacity, rows_here).transpose(1, 0, 2, 3)
-    scale_grid = scales.T.reshape(groups, per_dev, 1, rows_here).transpose(1, 0, 2, 3)
-    weighted = placement * scale_grid
     place_bf16 = placement.astype(jnp.bfloat16)
     outgoing = jnp.einsum(
         "enct,td->encd", place_bf16, tokens, preferred_element_type=jnp.float32
@@ -43,11 +41,12 @@
     )
     result = result.reshape(per_dev, groups, capacity, model_width)
     returned = lax.all_to_all(result, "expert", split_axis=1, concat_axis=1, tiled=True)
-    combined = jnp.einsum(
-        "enct,encd->td", weighted, returned.astype(jnp.float32), precision=lax.Precision.HIGHEST
-    ).astype(jnp.bfloat16)
+    combined = (weight * jnp.einsum(
+        "enct,encd->td", place_bf16, returned, preferred_element_type=jnp.float32
+    )).astype(jnp.bfloat16)
+    grad_out = (weight * cotangent.astype(jnp.float32)).astype(jnp.bfloat16)
     scaled_grad = jnp.einsum(
-        "enct,td->encd", weighted, cotangent.astype(jnp.float32), precision=lax.Precision.HIGHEST
+        "enct,td->encd", place_bf16, grad_out, preferred_element_type=jnp.float32
     ).astype(jnp.bfloat16)
     grad_rows = lax.all_to_all(
         scaled_grad, "expert", split_axis=1, concat_axis=1, tiled=True
@@ -68,9 +67,8 @@
     local_up = jnp.einsum("erd,erf->edf", incoming, grad_up_pre, preferred_element_type=jnp.float32)
     local_down = jnp.einsum("erf,erd->efd", hidden, grad_rows, preferred_element_type=jnp.float32)
     grad_gate, grad_up, grad_down = (
-        lax.psum_scatter(local_gate, "dp", scatter_dimension=1, tiled=True),
-        lax.psum_scatter(local_up, "dp", scatter_dimension=1, tiled=True),
-        lax.psum_scatter(local_down, "dp", scatter_dimension=2, tiled=True),
+        lax.psum_scatter(part.astype(jnp.bfloat16), "dp", scatter_dimension=dim, tiled=True).astype(jnp.float32)
+        for part, dim in ((local_gate, 1), (local_up, 1), (local_down, 2))
     )
     grad_back = lax.all_to_all(grad_input, "expert", split_axis=1, concat_axis=1, tiled=True)
     grad_tokens = jnp.einsum(

time: 388 us -> 393 us (1.013)
  local copies, waits for them, and re-layouts: 0.84 us -> 25.2 us
  waiting for transfers between devices: 295 us -> 274 us
  other arithmetic: 0.87 us -> 5.11 us
  matrix products: 54.2 us -> 50 us
    unnamed x8 -> x12, local copies, waits for them, and re-layouts: 0.84 us -> 23.7 us
    reduce_scatter x3 -> x2, waiting for transfers between devices: 156 us -> 140 us  [local(): lax.psum_scatter(part.astype(jnp.bfloat16), 'dp', scatter_dimension=dim,...]
    all_to_all x1, starting transfers between devices: 4.29 us -> 9.98 us  [local(): lax.all_to_all(scaled_grad, 'expert', split_axis=1, concat_axis=1, tiled=...]
    all_to_all x1, starting transfers between devices: 9.98 us -> 4.3 us  [local(): lax.all_to_all(outgoing, 'expert', split_axis=1, concat_axis=1, tiled=True)]
    all_to_all x1, waiting for transfers between devices: 33.9 us -> 28.5 us  [local(): lax.all_to_all(grad_input, 'expert', split_axis=1, concat_axis=1, tiled=T...]
    convert_element_type x0 -> x4, other arithmetic: none -> 5.11 us  [the longest x3 5.1 us: local(): lax.psum_scatter(part.astype(jnp.bfloat16), 'dp', scatter_dimension=dim,...]
where the time goes in v1:
time: 393 us; the launch traced here: 391 us
  waiting for transfers between devices  274 us (70%)
  matrix products  50 us (13%)
  local copies, waits for them, and re-layouts  25.2 us (6%)
  starting transfers between devices  23.2 us (6%)
  between operations  13.8 us (4%)
  other arithmetic  5.11 us (1%)
    reduce_scatter x2, waiting for transfers between devices, local(): lax.psum_scatter(part.astype(jnp.bfloat16), 'dp', scatter_dimension=dim,...  140 us
    all_to_all x1, waiting for transfers between devices, local(): lax.all_to_all(result, 'expert', split_axis=1, concat_axis=1, tiled=True)  35.8 us
    all_to_all x1, waiting for transfers between devices, local(): lax.all_to_all(scaled_grad, 'expert', split_axis=1, concat_axis=1, tiled=...  35.8 us
    all_to_all x1, waiting for transfers between devices, local(): lax.all_to_all(outgoing, 'expert', split_axis=1, concat_axis=1, tiled=True)  33.6 us
    all_to_all x1, waiting for transfers between devices, local(): lax.all_to_all(grad_input, 'expert', split_axis=1, concat_axis=1, tiled=T...  28.5 us
    unnamed x12, local copies, waits for them, and re-layouts  23.7 us
    all_to_all x1, starting transfers between devices, local(): lax.all_to_all(scaled_grad, 'expert', split_axis=1, concat_axis=1, tiled=...  9.98 us
  transfers between devices with their start and end apart: 7, of which 6 were waited for; matrix products, arithmetic and copies ran while one was open for 10% of the time, Pallas kernels for 0%

profile of v1, /device:TPU:1, one launch (start us, length us, event | category | flops | bytes accessed | tf_op | source)
XLA Modules:
  0.0 391.0 jit_solution(1331968550589832448)
XLA Ops:
  7.2 0.0 copy-start
  7.2 0.8 slice_bitcast_fusion
  8.0 0.2 fusion.45
  8.3 0.7 slice_bitcast_fusion.1
  9.0 2.8 fusion.21
  11.8 10.0 %all-to-all-start.2 = ((bf16[1,16,24,2048]{3,2,0,1:T(8,128)(2,1)}), bf16[1,16,24,2048]{3,2,0,1:T(8,128)(2,1)}, u32[]{:S(2)}, u32[]{:S(2)}) async-start(bf16[1,16,24,2048]{3,2,0,1:T(8,128)(2,1)} %fusion.21), calls=%async_computation.2 | async-start | bytes 3145728 | tf_op jit(solution)/shard_map/all_to_all | solution.py:51
  21.8 2.7 fusion.20
  24.5 35.8 %all-to-all-done.2 = bf16[1,16,24,2048]{3,2,0,1:T(8,128)(2,1)} async-done(((bf16[1,16,24,2048]{3,2,0,1:T(8,128)(2,1)}), bf16[1,16,24,2048]{3,2,0,1:T(8,128)(2,1)}, u32[]{:S(2)}, u32[]{:S(2)}) %all-to-all-start.2) | async-done | bytes 1572896 | tf_op jit(solution)/shard_map/all_to_all | solution.py:51
  60.3 4.3 %all-to-all-start = ((bf16[1,16,24,2048]{3,2,0,1:T(8,128)(2,1)}), bf16[1,16,24,2048]{3,2,0,1:T(8,128)(2,1)}, u32[]{:S(2)}, u32[]{:S(2)}) async-start(bf16[1,16,24,2048]{3,2,0,1:T(8,128)(2,1)} %fusion.20), calls=%async_computation | async-start | bytes 3145728 | tf_op jit(solution)/shard_map/all_to_all | solution.py:31
  64.6 0.0 reduce-scatter.10.cloned.1.call-start
  64.7 4.8 %fusion = f32[384,768]{1,0:T(8,128)} fusion(bf16[384,2048]{1,0:T(8,128)(2,1)} %bitcast.16, bf16[1,768,2048]{2,1,0:T(8,128)(2,1)} %param.12), kind=kOutput, calls=%fused_computation.4 | convolution fusion | flops 1207959552 | bytes 5898240 | tf_op jit(solution)/shard_map/erd,efd->erf/dot_general | solution.py:54
  69.5 33.6 %all-to-all-done = bf16[1,16,24,2048]{3,2,0,1:T(8,128)(2,1)} async-done(((bf16[1,16,24,2048]{3,2,0,1:T(8,128)(2,1)}), bf16[1,16,24,2048]{3,2,0,1:T(8,128)(2,1)}, u32[]{:S(2)}, u32[]{:S(2)}) %all-to-all-start) | async-done | bytes 1572896 | tf_op jit(solution)/shard_map/all_to_all | solution.py:31
  103.1 0.0 copy-start.2
  103.1 3.8 fusion.6
  107.0 0.0 copy-done
  107.0 0.0 copy-done.2
  107.0 4.2 %multiply_convert_fusion.1 = (bf16[384,768]{1,0:T(8,128)(2,1)}, bf16[384,768]{1,0:T(8,128)(2,1)}, bf16[384,768]{1,0:T(8,128)(2,1)S(1)}) fusion(f32[384,768]{1,0:T(8,128)S(1)} %copy-done.2, f32[384,768]{1,0:T(8,128)S(1)} %fusion.6, bf16[384,2048]{1,0:T(8,128)(2,1)} %bitcast.5, bf16[1,2048,768]{2,1,0:T(8,128)(2,1)S(1)} %copy-done), kind=kOutput, calls=%fused_computation.33 | convolution fusion | flops 1212383232 | bytes 8847360 | tf_op jit(solution)/shard_map/erd,edf->erf/dot_general | solution.py:34
  111.2 0.0 copy-start.3
  111.2 0.8 copy-done.3
  112.0 5.0 %fusion.14 = bf16[1,768,2048]{2,1,0:T(8,128)(2,1)} fusion(bf16[384,768]{1,0:T(8,128)(2,1)S(1)} %get-tuple-element.7, bf16[384,2048]{1,0:T(8,128)(2,1)} %bitcast.16), kind=kOutput, calls=%fused_computation.19 | convolution fusion | flops 1209532416 | bytes 5308416 | tf_op jit(solution)/shard_map/erf,erd->efd/dot_general | solution.py:68
  117.0 15.7 %copy.16 = bf16[1,768,2048]{1,0,2:T(2,128)(2,1)} copy(bf16[1,768,2048]{2,1,0:T(8,128)(2,1)} %fusion.14) | data formatting | bytes 6291456
  132.7 5.0 %copy.20 = bf16[2048,1,768]{2,0,1:T(8,128)(2,1)} copy(bf16[2048,1,768]{2,1,0:T(2,128)(2,1)} %bitcast.87) | data formatting | bytes 6291456
  137.7 0.0 reduce-scatter.10.cloned.1.call-update
  137.8 0.0 reduce-scatter.6.cloned.1.call-start
  137.8 5.0 %fusion.12 = bf16[1,2048,768]{2,1,0:T(8,128)(2,1)} fusion(bf16[384,2048]{1,0:T(8,128)(2,1)} %bitcast.5, bf16[384,768]{1,0:T(8,128)(2,1)} %get-tuple-element.5), kind=kOutput, calls=%fused_computation.17 | convolution fusion | flops 1209532416 | bytes 5308416 | tf_op jit(solution)/shard_map/erd,erf->edf/dot_general | solution.py:64
  142.8 0.0 reduce-scatter.6.cloned.1.call-update
  142.9 0.0 copy-start.1
  142.9 3.5 fusion.4
  146.4 0.0 copy-done.1
  146.4 2.6 add_convert_fusion
  149.0 4.3 %all-to-all-start.3 = ((bf16[1,16,24,2048]{3,2,0,1:T(8,128)(2,1)}), bf16[1,16,24,2048]{3,2,0,1:T(8,128)(2,1)}, u32[]{:S(2)}, u32[]{:S(2)}) async-start(bf16[1,16,24,2048]{3,2,0,1:T(8,128)(2,1)} %bitcast.89), calls=%async_computation.3 | async-start | bytes 3145728 | tf_op jit(solution)/shard_map/all_to_all | solution.py:73
  153.3 0.2 reduce-scatter.8.cloned.1.call-start
  153.5 5.0 %fusion.13 = bf16[1,2048,768]{2,1,0:T(8,128)(2,1)} fusion(bf16[384,2048]{1,0:T(8,128)(2,1)} %bitcast.5, bf16[384,768]{1,0:T(8,128)(2,1)} %get-tuple-element.6), kind=kOutput, calls=%fused_computation.18 | convolution fusion | flops 1209532416 | bytes 5308416 | tf_op jit(solution)/shard_map/erd,erf->edf/dot_general | solution.py:67
  158.6 0.0 reduce-scatter.8.cloned.1.call-update
  158.6 4.7 %fusion.17 = bf16[384,2048]{1,0:T(8,128)(2,1)} fusion(bf16[384,768]{1,0:T(8,128)(2,1)} %copy-done.3, bf16[1,768,2048]{2,1,0:T(8,128)(2,1)} %param.12), kind=kOutput, calls=%fused_computation.20 | convolution fusion | flops 1208745984 | bytes 5308416 | tf_op jit(solution)/shard_map/erf,efd->erd/dot_general | solution.py:39
  163.3 28.5 %all-to-all-done.3 = bf16[1,16,24,2048]{3,2,0,1:T(8,128)(2,1)} async-done(((bf16[1,16,24,2048]{3,2,0,1:T(8,128)(2,1)}), bf16[1,16,24,2048]{3,2,0,1:T(8,128)(2,1)}, u32[]{:S(2)}, u32[]{:S(2)}) %all-to-all-start.3) | async-done | bytes 1572896 | tf_op jit(solution)/shard_map/all_to_all | solution.py:73
  191.8 4.3 %all-to-all-start.1 = ((bf16[1,16,24,2048]{3,2,0,1:T(8,128)(2,1)}), bf16[1,16,24,2048]{3,2,0,1:T(8,128)(2,1)}, u32[]{:S(2)}, u32[]{:S(2)}) async-start(bf16[1,16,24,2048]{3,2,0,1:T(8,128)(2,1)} %bitcast.90), calls=%async_computation.1 | async-start | bytes 3145728 | tf_op jit(solution)/shard_map/all_to_all | solution.py:43
  196.1 2.7 fusion.24
  198.8 35.8 %all-to-all-done.1 = bf16[1,16,24,2048]{3,2,0,1:T(8,128)(2,1)} async-done(((bf16[1,16,24,2048]{3,2,0,1:T(8,128)(2,1)}), bf16[1,16,24,2048]{3,2,0,1:T(8,128)(2,1)}, u32[]{:S(2)}, u32[]{:S(2)}) %all-to-all-start.1) | async-done | bytes 1572896 | tf_op jit(solution)/shard_map/all_to_all | solution.py:43
  234.6 2.7 fusion.23
  237.3 0.0 reduce-scatter.10.cloned.1.call-done
  237.3 1.1 reshape_bitcast_fusion
  238.4 1.0 copy.17
  239.4 1.7 convert_element_type.113
  241.1 57.8 %reduce-scatter.6.cloned.1.call-done = bf16[1,128,768]{2,1,0:T(8,128)(2,1)} async-done(((bf16[1,2048,768]{2,1,0:T(8,128)(2,1)}), bf16[1,128,768]{2,1,0:T(8,128)(2,1)}) %reduce-scatter.6.cloned.1.call-update) | async-done | bytes 196624 | tf_op jit(solution)/shard_map/reduce_scatter | solution.py:70
  298.9 1.7 convert_element_type.107
  300.6 82.1 %reduce-scatter.8.cloned.1.call-done = bf16[1,128,768]{2,1,0:T(8,128)(2,1)} async-done(((bf16[1,2048,768]{2,1,0:T(8,128)(2,1)}), bf16[1,128,768]{2,1,0:T(8,128)(2,1)}) %reduce-scatter.8.cloned.1.call-update) | async-done | bytes 196624 | tf_op jit(solution)/shard_map/reduce_scatter | solution.py:70
  382.7 1.7 convert_element_type.110
  (1 shorter events, 0.0 us)
Async XLA Ops:
  7.2 99.8 %copy-start = (bf16[1,2048,768]{2,1,0:T(8,128)(2,1)S(1)}, bf16[1,2048,768]{2,1,0:T(8,128)(2,1)}, u32[]{:S(2)}) copy-start(bf16[1,2048,768]{2,1,0:T(8,128)(2,1)} %param.10) | copy-start | bytes 9437188
  11.8 48.5 %all-to-all-start.2 = ((bf16[1,16,24,2048]{3,2,0,1:T(8,128)(2,1)}), bf16[1,16,24,2048]{3,2,0,1:T(8,128)(2,1)}, u32[]{:S(2)}, u32[]{:S(2)}) async-start(bf16[1,16,24,2048]{3,2,0,1:T(8,128)(2,1)} %fusion.21), calls=%async_computation.2 | async-start | bytes 3145728 | tf_op jit(solution)/shard_map/all_to_all | solution.py:51
  60.3 42.8 %all-to-all-start = ((bf16[1,16,24,2048]{3,2,0,1:T(8,128)(2,1)}), bf16[1,16,24,2048]{3,2,0,1:T(8,128)(2,1)}, u32[]{:S(2)}, u32[]{:S(2)}) async-start(bf16[1,16,24,2048]{3,2,0,1:T(8,128)(2,1)} %fusion.20), calls=%async_computation | async-start | bytes 3145728 | tf_op jit(solution)/shard_map/all_to_all | solution.py:31
  64.6 172.7 %reduce-scatter.10.cloned.1.call-start = ((), (), s32[]{:S(2)}) async-start(), calls=%async_computation.9 | async-start | bytes 3342336
  103.1 3.9 copy-start.2
  111.2 0.8 copy-start.3
  137.8 161.1 %reduce-scatter.6.cloned.1.call-start = ((), (), s32[]{:S(2)}) async-start(), calls=%async_computation.7 | async-start | bytes 3342336 | tf_op jit(solution)/shard_map/reduce_scatter | solution.py:70
  142.9 3.6 copy-start.1
  149.0 42.8 %all-to-all-start.3 = ((bf16[1,16,24,2048]{3,2,0,1:T(8,128)(2,1)}), bf16[1,16,24,2048]{3,2,0,1:T(8,128)(2,1)}, u32[]{:S(2)}, u32[]{:S(2)}) async-start(bf16[1,16,24,2048]{3,2,0,1:T(8,128)(2,1)} %bitcast.89), calls=%async_computation.3 | async-start | bytes 3145728 | tf_op jit(solution)/shard_map/all_to_all | solution.py:73
  153.3 229.4 %reduce-scatter.8.cloned.1.call-start = ((), (), s32[]{:S(2)}) async-start(), calls=%async_computation.8 | async-start | bytes 3342336 | tf_op jit(solution)/shard_map/reduce_scatter | solution.py:70
  191.8 42.8 %all-to-all-start.1 = ((bf16[1,16,24,2048]{3,2,0,1:T(8,128)(2,1)}), bf16[1,16,24,2048]{3,2,0,1:T(8,128)(2,1)}, u32[]{:S(2)}, u32[]{:S(2)}) async-start(bf16[1,16,24,2048]{3,2,0,1:T(8,128)(2,1)} %bitcast.90), calls=%async_computation.1 | async-start | bytes 3145728 | tf_op jit(solution)/shard_map/all_to_all | solution.py:43
Sparse Core Ops, SparseCore 0:
  137.9 77.4 reduce-scatter.9
  219.1 79.7 reduce-scatter.5
  302.5 80.1 reduce-scatter.7

commit v2 on v1

v2 whole, which is shorter than its diff:
```python
import functools

import jax
import jax.numpy as jnp
from jax import lax
from jax.experimental import pallas as pl
from jax.experimental.pallas import tpu as pltpu
from jax.sharding import PartitionSpec as P

CAP = 24
MESH = pl.DeviceIdType.MESH
F32, BF16 = jnp.float32, jnp.bfloat16
HOPS = (128, 128, 80, 32)
OFFS = (0, HOPS[0], HOPS[0] + HOPS[1], HOPS[0] + HOPS[1] + HOPS[2])
ROWS = sum(HOPS)
PAIR = 8 * CAP
TOK, COT = 0, 1
COLS = 512


def dot(a, b, ca=1, cb=0):
    return lax.dot_general(a, b, (((ca,), (cb,)), ((), ())), preferred_element_type=F32)


def kernel(
    with_dp, ids_ref, idst_ref, gw_ref, tok_ref, cot_ref, wg_hbm, wu_hbm, wd_hbm,
    comb_ref, gtok_ref, gg_ref, gu_ref, gd_ref,
    wg, wu, wd, gdn, own, ring, back, meta, sel, sel0, place, work, away, out, near, pre, hid, dgu, rs0, rs1,
    w_sem, z_send, z_recv, m_send, m_recv, p_send, p_recv, r_send, r_recv,
):
    rows, width = tok_ref.shape
    ff = hid.shape[1]
    half = ff // 2
    dp, ex = lax.axis_index("dp"), lax.axis_index("expert")
    core = lax.rem(ex, 2)
    z = lax.div(ex, 2)
    px, py = lax.rem(dp, 4), lax.div(dp, 4)

    def at_z(step):
        return (dp, lax.rem(z + step + 8, 8) * 2 + core)

    partner = (dp, z * 2 + 1 - core)

    def at_dp(axis, step):
        if axis == 0:
            return (py * 4 + lax.rem(px + step + 4, 4), ex)
        return (lax.rem(py + step + 4, 4) * 4 + px, ex)

    loads = [
        pltpu.make_async_copy(wg_hbm, wg, w_sem.at[0]),
        pltpu.make_async_copy(wu_hbm, wu, w_sem.at[1]),
        pltpu.make_async_copy(wd_hbm, wd, w_sem.at[2]),
    ]
    for load in loads:
        load.start()

    neighbours = [at_z(1), at_z(-1), partner]
    if with_dp:
        neighbours += [at_dp(0, 1), at_dp(0, -1), at_dp(1, 1), at_dp(1, -1)]
    barrier = pltpu.get_barrier_semaphore()
    for device in neighbours:
        pl.semaphore_signal(barrier, inc=1, device_id=device, device_id_type=MESH)

    def keys(e):
        odd = e & 1
        d = ((e >> 1) - z) & 7
        plus = jnp.where((d >= 1) & (d <= 3), d, jnp.where((d == 4) & (odd == 0), 4, 0))
        minus = jnp.where(d >= 5, 8 - d, jnp.where((d == 4) & (odd == 1), 4, 0))
        return odd, d, (plus, minus)

    e_c, e_r = ids_ref[:, 0:1], idst_ref[0:1, :]
    odd_c, _, key_c = keys(e_c)
    odd_r, d_r, key_r = keys(e_r)
    i0 = lax.broadcasted_iota(jnp.int32, (rows, rows), 0)
    i1 = lax.broadcasted_iota(jnp.int32, (rows, rows), 1)
    same = e_c == e_r
    rank_c = jnp.sum((same & (i1 < i0)).astype(F32), axis=1, keepdims=True)
    rank_r = jnp.sum((same & (i0 < i1)).astype(F32), axis=0, keepdims=True)
    for s in range(2):
        ahead = (key_r[s] > key_c[s]) | ((key_r[s] == key_c[s]) & (i1 < i0))
        pos = jnp.sum(ahead.astype(F32), axis=1, keepdims=True)
        hit = pos == i1.astype(F32)
        place[s] = hit.astype(BF16)
        code = jnp.where(key_c[s] > 0, (64 * key_c[s] + 24 * odd_c).astype(F32) + rank_c, 0.0)
        row = jnp.sum(jnp.where(hit, code, 0.0), axis=0, keepdims=True)
        meta[s, 0] = jnp.broadcast_to(row, meta.shape[2:])

    j = lax.broadcasted_iota(jnp.int32, (96, rows), 0)
    other = j >= 48
    j = jnp.where(other, j - 48, j)
    second = j >= CAP
    j = jnp.where(second, j - CAP, j)
    slot = (j + CAP * jnp.where(other, 1 - core, core)).astype(F32)
    slot_a = jnp.where(second, -9.0, slot)
    slot_b = jnp.where(second, slot, -9.0)
    code0 = jnp.where(d_r == 0, (24 * odd_r).astype(F32) + rank_r, -5.0)
    sel0[...] = (code0 == slot_a).astype(BF16)

    def tiles(n, body):
        def step(i, carry):
            body(i)
            return carry
        lax.fori_loop(0, n, step, 0)

    n_cols = width // COLS

    def cols(i):
        return pl.ds(pl.multiple_of(i * COLS, COLS), COLS)

    def build(kind, source):
        def body(i):
            block = source[:, cols(i)]
            for s in range(2):
                own[kind, s, :, cols(i)] = dot(place[s, :, : HOPS[0]], block, 0, 0).astype(BF16)
        tiles(n_cols, body)

    sends = []

    def send(src, dst, ssem, rsem, device, keep=True):
        copy = pltpu.make_async_remote_copy(
            src_ref=src, dst_ref=dst, send_sem=ssem, recv_sem=rsem, device_id=device, device_id_type=MESH
        )
        copy.start()
        if keep:
            sends.append(copy)
        return copy

    def part(ref, kind, s, h, n=None):
        return ref.at[kind, s, pl.ds(OFFS[h - 1], HOPS[h - 1] if n is None else n)]

    metas, moves = {}, {}

    def forward_meta(h):
        for s, step in ((0, 1), (1, -1)):
            metas[s, h] = send(
                meta.at[s, h - 1], meta.at[s, h], m_send.at[s, h - 1], m_recv.at[s, h - 1], at_z(step)
            )

    def forward(kind, h):
        for s, step in ((0, 1), (1, -1)):
            src = own.at[kind, s] if h == 1 else part(ring, kind, s, h - 1, HOPS[h - 1])
            moves[kind, s, h] = send(
                src, part(ring, kind, s, h), z_send.at[kind, s, h - 1], z_recv.at[kind, s, h - 1], at_z(step),
                keep=False,
            )

    def arrived(kind, h):
        for s in range(2):
            moves[kind, s, h].wait_recv()

    def choose(h):
        for s in range(2):
            metas[s, h].wait_recv()
        for s in range(2):
            slots = slot_b if s == 1 or h == 4 else slot_a
            sel[s, h - 1] = ((meta[s, h, 0:1, :] - 64.0 * h) == slots).astype(BF16)

    def select(kind, h):
        g = h % 4
        lo, n = OFFS[h - 1], HOPS[h - 1]
        source = (tok_ref, cot_ref)[kind]

        def body(i):
            total = dot(sel[0, h - 1, :, :n], ring[kind, 0, lo : lo + n, cols(i)]) + dot(
                sel[1, h - 1, :, :n], ring[kind, 1, lo : lo + n, cols(i)]
            )
            if h == 4:
                total = total + dot(sel0[...], source[:, cols(i)])
            total = total.astype(BF16)
            work[kind, 48 * g : 48 * g + 48, cols(i)] = total[:48]
            away[kind, 48 * g : 48 * g + 48, cols(i)] = total[48:]

        tiles(n_cols, body)

    pairs = {}

    def swap_in(kind):
        pairs[kind] = send(
            away.at[kind], work.at[kind, pl.ds(PAIR, PAIR)], p_send.at[kind], p_recv.at[kind], partner
        )

    def swap_out(kind):
        pairs[2 + kind] = send(
            out.at[kind, pl.ds(PAIR, PAIR)], near.at[kind], p_send.at[2 + kind], p_recv.at[2 + kind], partner
        )

    def group(kind, g, i):
        return jnp.concatenate(
            [out[kind, 48 * g : 48 * g + 48, cols(i)], near[kind, 48 * g : 48 * g + 48, cols(i)]], axis=0
        )

    backs = {}

    def give_back(kind, h):
        if h < 4:
            for s in range(2):
                backs[kind, s, h + 1].wait_recv()
        lo, n = OFFS[h - 1], HOPS[h - 1]

        def body(i):
            results = group(kind, h % 4, i)
            for s in range(2):
                total = dot(sel[s, h - 1, :, :n], results, 0, 0)
                if h < 4:
                    far, m = OFFS[h], HOPS[h]
                    ring[kind, s, lo : lo + m, cols(i)] = (
                        total[:m] + back[kind, s, far : far + m, cols(i)].astype(F32)
                    ).astype(BF16)
                    if m < n:
                        ring[kind, s, lo + m : lo + n, cols(i)] = total[m:].astype(BF16)
                else:
                    ring[kind, s, lo : lo + n, cols(i)] = total.astype(BF16)

        tiles(n_cols, body)
        for s, step in ((0, -1), (1, 1)):
            backs[kind, s, h] = send(
                part(ring, kind, s, h), part(back, kind, s, h),
                z_send.at[2 + kind, s, h - 1], z_recv.at[2 + kind, s, h - 1], at_z(step),
            )

    def deliver(kind, target):
        for s in range(2):
            backs[kind, s, 1].wait_recv()

        def body(i):
            total = dot(sel0[...], group(kind, 0, i), 0, 0)
            for s in range(2):
                total = total + dot(place[s, :, : HOPS[0]], back[kind, s, : HOPS[0], cols(i)])
            target[:, cols(i)] = total.astype(BF16)

        tiles(n_cols, body)

    grads = (gdn, wg, wu)
    results = (gd_ref, gg_ref, gu_ref)
    sums = {}

    def place_of(stage, side):
        axis = side if stage == 0 else 1 - side
        return axis, (px, py)[axis]

    def view(m, stage, side, dest, upper):
        c = slice(side * half, (side + 1) * half)
        if stage == 0:
            many = slice(2 * upper, 2 * upper + 2)
            return (many, dest, slice(None), c) if side == 0 else (dest, many, slice(None), c)
        many = slice(64 * upper, 64 * upper + 64)
        return (dest, px, many, c) if side == 0 else (py, dest, many, c)

    def rs_send(m, stage, side, slot):
        axis, p = place_of(stage, side)
        dest, upper, step = (
            (2, 0, 1), (1, 1, 1), (1, 0, 1), (2, 1, -1), (3, 0, -1), (3, 1, -1)
        )[slot]
        where = view(m, stage, side, lax.rem(p + dest, 4), upper)
        sums[m, stage, side, slot] = send(
            grads[m].at[where], (rs0, rs1)[stage].at[m, side, slot],
            r_send.at[m, stage, side, slot], r_recv.at[m, stage, side, slot], at_dp(axis, step),
        )

    def rs_got(m, stage, side, slot):
        sums[m, stage, side, slot].wait_recv()
        return (rs0, rs1)[stage][m, side, slot].astype(F32)

    def rs_start(m, stage):
        for slot in (0, 3, 1, 4):
            for side in range(2):
                rs_send(m, stage, side, slot)

    def rs_relay(m, stage):
        for far, dest, upper in ((0, 1, 0), (3, 3, 1)):
            for side in range(2):
                _, p = place_of(stage, side)
                where = view(m, stage, side, lax.rem(p + dest, 4), upper)
                grads[m][where] = (grads[m][where].astype(F32) + rs_got(m, stage, side, far)).astype(BF16)
                rs_send(m, stage, side, far + 2)

    def rs_finish(m, stage):
        for upper, (a, b) in enumerate(((4, 2), (1, 5))):
            for side in range(2):
                _, p = place_of(stage, side)
                where = view(m, stage, side, p, upper)
                total = grads[m][where].astype(F32) + rs_got(m, stage, side, a) + rs_got(m, stage, side, b)
                if stage == 0:
                    grads[m][where] = total.astype(BF16)
                else:
                    results[m][64 * upper : 64 * upper + 64, side * half : (side + 1) * half] = total

    build(TOK, tok_ref)
    pl.semaphore_wait(barrier, len(neighbours))
    forward_meta(1)
    forward(TOK, 1)
    build(COT, cot_ref)
    forward(COT, 1)
    for h in (1, 2, 3):
        choose(h)
        forward_meta(h + 1)
        arrived(TOK, h)
        forward(TOK, h + 1)
        arrived(COT, h)
        forward(COT, h + 1)
        select(TOK, h)
        select(COT, h)
    choose(4)
    arrived(TOK, 4)
    select(TOK, 4)
    swap_in(TOK)
    for load in loads:
        load.wait()
    pairs[TOK].wait_recv()

    def ff_tile(i):
        return pl.ds(pl.multiple_of(i * 256, 256), 256)

    def up_body(i):
        x = work[TOK]
        gate = dot(x, wg[:, :, :, ff_tile(i)].reshape(width, 256))
        up = dot(x, wu[:, :, :, ff_tile(i)].reshape(width, 256))
        pre[0, :, ff_tile(i)] = gate
        pre[1, :, ff_tile(i)] = up
        hid[:, ff_tile(i)] = (gate * jax.nn.sigmoid(gate) * up).astype(BF16)

    tiles(ff // 256, up_body)

    def down_body(i):
        out[TOK, :, cols(i)] = dot(hid[...], wd[:, cols(i)]).astype(BF16)

    tiles(n_cols, down_body)
    swap_out(TOK)

    arrived(COT, 4)
    select(COT, 4)
    swap_in(COT)
    for kind in (TOK, COT):
        for h in (1, 2, 3, 4):
            for s in range(2):
                moves[kind, s, h].wait_send()
    pairs[2 + TOK].wait_recv()
    give_back(TOK, 4)
    pairs[COT].wait_recv()

    def down_grad(i):
        gdn[i] = dot(work[COT, :, cols(i)], hid[...], 0, 0).astype(BF16).reshape(4, 128, ff)

    tiles(n_cols, down_grad)
    if with_dp:
        rs_start(0, 0)
    give_back(TOK, 3)

    def grad_body(i):
        gh = dot(work[COT], wd[ff_tile(i), :], 1, 1)
        gate, up = pre[0, :, ff_tile(i)], pre[1, :, ff_tile(i)]
        s = jax.nn.sigmoid(gate)
        dgu[:, ff_tile(i)] = (gh * up * s * (1.0 + gate * (1.0 - s))).astype(BF16)
        dgu[:, pl.ds(pl.multiple_of(ff + i * 256, 256), 256)] = (gh * (gate * s)).astype(BF16)

    tiles(ff // 256, grad_body)
    give_back(TOK, 2)

    def in_grad(i):
        total = dot(dgu[:, :ff], wg[i].reshape(COLS, ff), 1, 1) + dot(dgu[:, ff:], wu[i].reshape(COLS, ff), 1, 1)
        out[COT, :, cols(i)] = total.astype(BF16)

    tiles(n_cols, in_grad)
    swap_out(COT)
    if with_dp:
        rs_relay(0, 0)

    def up_grad(i):
        x = work[TOK, :, cols(i)]
        wg[i] = dot(x, dgu[:, :ff], 0, 0).astype(BF16).reshape(4, 128, ff)
        wu[i] = dot(x, dgu[:, ff:], 0, 0).astype(BF16).reshape(4, 128, ff)

    tiles(n_cols, up_grad)
    if with_dp:
        rs_start(1, 0)
        rs_start(2, 0)
    pairs[2 + COT].wait_recv()
    give_back(COT, 4)
    give_back(TOK, 1)
    give_back(COT, 3)
    if with_dp:
        rs_finish(0, 0)
        rs_start(0, 1)
        rs_relay(1, 0)
        rs_relay(2, 0)
        rs_relay(0, 1)
    give_back(COT, 2)
    if with_dp:
        rs_finish(1, 0)
        rs_start(1, 1)
    give_back(COT, 1)
    if with_dp:
        rs_finish(0, 1)
        rs_finish(2, 0)
        rs_start(2, 1)
        rs_relay(1, 1)
        rs_relay(2, 1)
    deliver(TOK, comb_ref)
    if with_dp:
        rs_finish(1, 1)
        rs_finish(2, 1)
    else:
        for ref in results:
            ref[...] = jnp.zeros_like(ref)
    deliver(COT, gtok_ref)
    for copy in sends:
        copy.wait_send()


def local(tokens, expert_ids, gate_weights, w_gate, w_up, w_down, cotangent):
    rows, width = tokens.shape
    ff = w_gate.shape[2]
    with_dp = lax.axis_size("dp") == 16
    shard = width // 16
    weight = gate_weights[:, :1]
    grad_out = (weight * cotangent.astype(F32)).astype(BF16)
    vmem, hbm = pl.BlockSpec(memory_space=pltpu.VMEM), pl.BlockSpec(memory_space=pl.ANY)
    dma = pltpu.SemaphoreType.DMA
    combined, grad_tokens, grad_gate, grad_up, grad_down = pl.pallas_call(
        functools.partial(kernel, with_dp),
        out_shape=(
            jax.ShapeDtypeStruct((rows, width), BF16),
            jax.ShapeDtypeStruct((rows, width), BF16),
            jax.ShapeDtypeStruct((shard, ff), F32),
            jax.ShapeDtypeStruct((shard, ff), F32),
            jax.ShapeDtypeStruct((shard, ff), F32),
        ),
        in_specs=[vmem] * 5 + [hbm] * 3,
        out_specs=(vmem,) * 5,
        scratch_shapes=[
            pltpu.VMEM((4, 4, shard, ff), BF16),
            pltpu.VMEM((4, 4, shard, ff), BF16),
            pltpu.VMEM((ff, width), BF16),
            pltpu.VMEM((4, 4, shard, ff), BF16),
            pltpu.VMEM((2, 2, HOPS[0], width), BF16),
            pltpu.VMEM((2, 2, ROWS, width), BF16),
            pltpu.VMEM((2, 2, ROWS, width), BF16),
            pltpu.VMEM((2, 5, 8, rows), F32),
            pltpu.VMEM((2, 4, 96, rows), BF16),
            pltpu.VMEM((96, rows), BF16),
            pltpu.VMEM((2, rows, rows), BF16),
            pltpu.VMEM((2, 2 * PAIR, width), BF16),
            pltpu.VMEM((2, PAIR, width), BF16),
            pltpu.VMEM((2, 2 * PAIR, width), BF16),
            pltpu.VMEM((2, PAIR, width), BF16),
            pltpu.VMEM((2, 2 * PAIR, ff), F32),
            pltpu.VMEM((2 * PAIR, ff), BF16),
            pltpu.VMEM((2 * PAIR, 2 * ff), BF16),
            pltpu.VMEM((3, 2, 6, 2, shard, ff // 2), BF16),
            pltpu.VMEM((3, 2, 6, shard // 2, ff // 2), BF16),
            dma((3,)),
            dma((4, 2, 4)),
            dma((4, 2, 4)),
            dma((2, 4)),
            dma((2, 4)),
            dma((4,)),
            dma((4,)),
            dma((3, 2, 2, 6)),
            dma((3, 2, 2, 6)),
        ],
        compiler_params=pltpu.CompilerParams(
            collective_id=0, has_side_effects=True, vmem_limit_bytes=63 * 2**20
        ),
    )(
        expert_ids, expert_ids.T, gate_weights, tokens, grad_out,
        w_gate.reshape(4, 4, shard, ff), w_up.reshape(4, 4, shard, ff), w_down.reshape(ff, width),
    )
    combined = (weight * combined.astype(F32)).astype(BF16)
    return (combined, grad_tokens, grad_gate[None], grad_up[None], grad_down.T[None])


def solution(mesh):
    in_specs = (
        P(("dp", "expert"), None),
        P(("dp", "expert"), None),
        P(("dp", "expert"), None),
        P("expert", None, None),
        P("expert", None, None),
        P("expert", None, None),
        P(("dp", "expert"), None),
    )
    out_specs = (
        P(("dp", "expert"), None),
        P(("dp", "expert"), None),
        P("expert", "dp", None),
        P("expert", "dp", None),
        P("expert", None, "dp"),
    )
    return jax.shard_map(local, mesh=mesh, in_specs=in_specs, out_specs=out_specs, check_vma=False)
```

time: 393 us -> 173 us (0.44)
  waiting for transfers between devices: 274 us -> 0 us
  Pallas kernels: 0 us -> 157 us
  matrix products: 50 us -> 0 us
  starting transfers between devices: 23.2 us -> 0 us
  local copies, waits for them, and re-layouts: 25.2 us -> 8.81 us
  between operations: 13.8 us -> 0.66 us
    pallas_call x0 -> x1, Pallas kernels: none -> 157 us  [local(): pl.pallas_call(functools.partial(kernel, with_dp), out_shape=(jax.ShapeDt...]
    reduce_scatter x2 -> x0, waiting for transfers between devices: 140 us -> none  [local(): lax.psum_scatter(part.astype(jnp.bfloat16), 'dp', scatter_dimension=dim,...]
    all_to_all x4 -> x0, waiting for transfers between devices: 134 us -> none  [the longest x1 35.8 us: local(): lax.all_to_all(result, 'expert', split_axis=1, concat_axis=1, tiled=True)]
    dot_general x14 -> x0, matrix products: 50 us -> none  [the longest x1 5.04 us: local(): jnp.einsum('erd,erf->edf', incoming, grad_up_pre, preferred_element_type=...]
    all_to_all x4 -> x0, starting transfers between devices: 22.9 us -> none  [the longest x1 9.98 us: local(): lax.all_to_all(scaled_grad, 'expert', split_axis=1, concat_axis=1, tiled=...]
    unnamed x12 -> x10, local copies, waits for them, and re-layouts: 23.7 us -> 8.12 us
  transfers between devices with their start and end apart: 7 -> 0, of which waited for: 6 -> 0; matrix products, arithmetic and copies ran while one was open for 10% -> 0% of each run, Pallas kernels for 0% -> 0%
where the time goes in v2:
time: 173 us; the launch traced here: 171 us
  Pallas kernels  157 us (91%)
  local copies, waits for them, and re-layouts  8.81 us (5%)
  other arithmetic  4.04 us (2%)
    pallas_call x1, Pallas kernels, local(): pl.pallas_call(functools.partial(kernel, with_dp), out_shape=(jax.ShapeDt...  157 us
    unnamed x10, local copies, waits for them, and re-layouts  8.12 us

profile of v2, /device:TPU:1, one launch (start us, length us, event | category | flops | bytes accessed | tf_op | source)
XLA Modules:
  0.0 170.7 jit_solution(15890963694763933194)
XLA Ops:
  0.6 0.7 slice_bitcast_fusion
  1.3 1.4 copy.12.ids_ref
  2.7 1.4 copy.13.gw_ref
  4.2 2.0 %multiply_convert_fusion.1.cot_ref = bf16[128,2048]{1,0:T(8,128)(2,1)} fusion(bf16[128,2048]{1,0:T(8,128)(2,1)} %param.13, f32[128]{0:T(128)S(1)} %slice_bitcast_fusion), kind=kLoop, calls=%fused_computation.1 | loop fusion | flops 786432 | bytes 1049088 | tf_op jit(solution)/shard_map/convert_element_type | solution.py:416
  6.1 157.2 %shard_map.110 = (bf16[128,2048]{1,0:T(8,128)(2,1)}, bf16[128,2048]{1,0:T(8,128)(2,1)}, f32[128,768]{1,0:T(8,128)}, f32[128,768]{1,0:T(8,128)}, f32[128,768]{1,0:T(8,128)}) custom-call(s32[128,8]{1,0:T(8,128)} %copy.12.ids_ref, s32[8,128]{1,0:T(8,128)} %bitcast.17, f32[128,8]{1,0:T(8,128)} %copy.13.gw_ref, bf16[128,2048]{1,0:T(8,128)(2,1)} %tok_ref.1, ...), custom_call_target="tpu_custom_call" | custom-call | tf_op jit(solution)/shard_map/pallas_call | solution.py:419
  163.4 0.0 copy-start.1
  163.4 0.0 copy-start
  163.4 2.1 %multiply_convert_fusion = bf16[128,2048]{1,0:T(8,128)(2,1)} fusion(bf16[128,2048]{1,0:T(8,128)(2,1)} %get-tuple-element.10, f32[128]{0:T(128)S(1)} %slice_bitcast_fusion), kind=kLoop, calls=%fused_computation | loop fusion | flops 786432 | bytes 1049088 | tf_op jit(solution)/shard_map/convert_element_type | solution.py:468
  165.4 1.9 %copy.14 = f32[1,768,128]{2,1,0:T(8,128)} copy(f32[1,768,128]{1,2,0:T(8,128)} %bitcast.16) | data formatting | bytes 786432
  167.4 1.9 %copy.18 = bf16[128,2048]{1,0:T(8,128)(2,1)} copy(bf16[128,2048]{1,0:T(8,128)(2,1)} %get-tuple-element.26) | data formatting | bytes 1048576
  169.2 0.0 copy-done.1
  169.2 0.7 copy.19
  170.0 0.0 copy-done
  170.0 0.7 copy.20
Async XLA Ops:
  163.4 5.9 %copy-start.1 = (f32[128,768]{1,0:T(8,128)S(1)}, f32[128,768]{1,0:T(8,128)}, u32[]{:S(2)}) copy-start(f32[128,768]{1,0:T(8,128)} %get-tuple-element.12) | copy-start | bytes 1179652
  163.4 6.6 %copy-start = (f32[128,768]{1,0:T(8,128)S(1)}, f32[128,768]{1,0:T(8,128)}, u32[]{:S(2)}) copy-start(f32[128,768]{1,0:T(8,128)} %get-tuple-element.13) | copy-start | bytes 1179652

commit v3 on v2

--- a/solution.py
+++ b/solution.py
@@ -10,7 +10,7 @@
 CAP = 24
 MESH = pl.DeviceIdType.MESH
 F32, BF16 = jnp.float32, jnp.bfloat16
-HOPS = (128, 128, 80, 32)
+HOPS = (128, 96, 64, 32)
 OFFS = (0, HOPS[0], HOPS[0] + HOPS[1], HOPS[0] + HOPS[1] + HOPS[2])
 ROWS = sum(HOPS)
 PAIR = 8 * CAP
@@ -23,9 +23,9 @@
 
 
 def kernel(
-    with_dp, ids_ref, idst_ref, gw_ref, tok_ref, cot_ref, wg_hbm, wu_hbm, wd_hbm,
+    with_dp, idst_ref, gwt_ref, tok_ref, cot_ref, wg_hbm, wu_hbm, wd_hbm,
     comb_ref, gtok_ref, gg_ref, gu_ref, gd_ref,
-    wg, wu, wd, gdn, own, ring, back, meta, sel, sel0, place, work, away, out, near, pre, hid, dgu, rs0, rs1,
+    wg, wu, wd, gdn, scaled, own, ring, back, meta, sel, sel0, place, work, away, out, near, pre, hid, dgu, rs0, rs1,
     w_sem, z_send, z_recv, m_send, m_recv, p_send, p_recv, r_send, r_recv,
 ):
     rows, width = tok_ref.shape
@@ -61,18 +61,35 @@
     for device in neighbours:
         pl.semaphore_signal(barrier, inc=1, device_id=device, device_id_type=MESH)
 
-    def keys(e):
-        odd = e & 1
-        d = ((e >> 1) - z) & 7
-        plus = jnp.where((d >= 1) & (d <= 3), d, jnp.where((d == 4) & (odd == 0), 4, 0))
-        minus = jnp.where(d >= 5, 8 - d, jnp.where((d == 4) & (odd == 1), 4, 0))
-        return odd, d, (plus, minus)
-
-    e_c, e_r = ids_ref[:, 0:1], idst_ref[0:1, :]
-    odd_c, _, key_c = keys(e_c)
-    odd_r, d_r, key_r = keys(e_r)
+    def distance(e):
+        return ((e >> 1) - z) & 7
+
     i0 = lax.broadcasted_iota(jnp.int32, (rows, rows), 0)
     i1 = lax.broadcasted_iota(jnp.int32, (rows, rows), 1)
+
+    def column(row):
+        return jnp.sum(jnp.where(i0 == i1, row, jnp.zeros_like(row)), axis=1, keepdims=True)
+
+    e_r = idst_ref[0:1, :]
+    e_c = column(e_r.astype(F32)).astype(jnp.int32)
+    weight = column(gwt_ref[0:1, :])
+    odd_c, odd_r = e_c & 1, e_r & 1
+    d_c, d_r = distance(e_c), distance(e_r)
+
+    def count(lo, hi):
+        return jnp.sum(((d_r >= lo) & (d_r <= hi)).astype(F32), axis=1, keepdims=True)
+
+    limit = jnp.minimum(jnp.minimum(HOPS[3], HOPS[2] - count(3, 3)), HOPS[1] - count(2, 3))
+    before_c = jnp.sum(((d_r == 4) & (i1 < i0)).astype(F32), axis=1, keepdims=True)
+    before_r = jnp.sum(((d_c == 4) & (i0 < i1)).astype(F32), axis=0, keepdims=True)
+
+    def keys(d, before):
+        first = before < limit
+        plus = jnp.where((d >= 1) & (d <= 3), d, jnp.where((d == 4) & first, 4, 0))
+        minus = jnp.where(d >= 5, 8 - d, jnp.where((d == 4) & ~first, 4, 0))
+        return plus, minus
+
+    key_c, key_r = keys(d_c, before_c), keys(d_r, before_r)
     same = e_c == e_r
     rank_c = jnp.sum((same & (i1 < i0)).astype(F32), axis=1, keepdims=True)
     rank_r = jnp.sum((same & (i0 < i1)).astype(F32), axis=0, keepdims=True)
@@ -107,9 +124,13 @@
     def cols(i):
         return pl.ds(pl.multiple_of(i * COLS, COLS), COLS)
 
-    def build(kind, source):
+    def build(kind):
         def body(i):
-            block = source[:, cols(i)]
+            if kind == TOK:
+                block = tok_ref[:, cols(i)]
+            else:
+                block = (weight * cot_ref[:, cols(i)].astype(F32)).astype(BF16)
+                scaled[:, cols(i)] = block
             for s in range(2):
                 own[kind, s, :, cols(i)] = dot(place[s, :, : HOPS[0]], block, 0, 0).astype(BF16)
         tiles(n_cols, body)
@@ -125,9 +146,6 @@
             sends.append(copy)
         return copy
 
-    def part(ref, kind, s, h, n=None):
-        return ref.at[kind, s, pl.ds(OFFS[h - 1], HOPS[h - 1] if n is None else n)]
-
     metas, moves = {}, {}
 
     def forward_meta(h):
@@ -136,17 +154,23 @@
                 meta.at[s, h - 1], meta.at[s, h], m_send.at[s, h - 1], m_recv.at[s, h - 1], at_z(step)
             )
 
-    def forward(kind, h):
+    def chunk(q, n):
+        return pl.ds(q * (width // n), width // n)
+
+    def forward(kind, h, q=0, n=1):
+        many = HOPS[h - 1]
         for s, step in ((0, 1), (1, -1)):
-            src = own.at[kind, s] if h == 1 else part(ring, kind, s, h - 1, HOPS[h - 1])
-            moves[kind, s, h] = send(
-                src, part(ring, kind, s, h), z_send.at[kind, s, h - 1], z_recv.at[kind, s, h - 1], at_z(step),
-                keep=False,
+            src = own.at[kind, s] if h == 1 else ring.at[kind, s, pl.ds(OFFS[h - 2], many)]
+            dst = ring.at[kind, s, pl.ds(OFFS[h - 1], many)]
+            if n > 1:
+                src, dst = src.at[:, chunk(q, n)], dst.at[:, chunk(q, n)]
+            moves[kind, s, h, q] = send(
+                src, dst, z_send.at[kind, s, h - 1, q], z_recv.at[kind, s, h - 1, q], at_z(step), keep=False
             )
 
-    def arrived(kind, h):
+    def arrived(kind, h, q=0):
         for s in range(2):
-            moves[kind, s, h].wait_recv()
+            moves[kind, s, h, q].wait_recv()
 
     def choose(h):
         for s in range(2):
@@ -158,7 +182,7 @@
     def select(kind, h):
         g = h % 4
         lo, n = OFFS[h - 1], HOPS[h - 1]
-        source = (tok_ref, cot_ref)[kind]
+        source = (tok_ref, scaled)[kind]
 
         def body(i):
             total = dot(sel[0, h - 1, :, :n], ring[kind, 0, lo : lo + n, cols(i)]) + dot(
@@ -174,15 +198,21 @@
 
     pairs = {}
 
-    def swap_in(kind):
-        pairs[kind] = send(
-            away.at[kind], work.at[kind, pl.ds(PAIR, PAIR)], p_send.at[kind], p_recv.at[kind], partner
+    def swap_in(kind, g):
+        pairs[kind, g] = send(
+            away.at[kind, pl.ds(48 * g, 48)], work.at[kind, pl.ds(PAIR + 48 * g, 48)],
+            p_send.at[kind, g], p_recv.at[kind, g], partner,
         )
 
-    def swap_out(kind):
-        pairs[2 + kind] = send(
-            out.at[kind, pl.ds(PAIR, PAIR)], near.at[kind], p_send.at[2 + kind], p_recv.at[2 + kind], partner
+    def swap_out(kind, i):
+        pairs[2 + kind, i] = send(
+            out.at[kind, pl.ds(PAIR, PAIR), chunk(i, 4)], near.at[kind, :, chunk(i, 4)],
+            p_send.at[2 + kind, i], p_recv.at[2 + kind, i], partner,
         )
+
+    def swapped(kind):
+        for i in range(4):
+            pairs[kind, i].wait_recv()
 
     def group(kind, g, i):
         return jnp.concatenate(
@@ -191,13 +221,17 @@
 
     backs = {}
 
-    def give_back(kind, h):
+    def give_back(kind, h, q):
         if h < 4:
             for s in range(2):
-                backs[kind, s, h + 1].wait_recv()
+                backs[kind, s, h + 1, q].wait_recv()
+        else:
+            for i in (2 * q, 2 * q + 1):
+                pairs[2 + kind, i].wait_recv()
         lo, n = OFFS[h - 1], HOPS[h - 1]
 
-        def body(i):
+        def body(k):
+            i = 2 * q + k
             results = group(kind, h % 4, i)
             for s in range(2):
                 total = dot(sel[s, h - 1, :, :n], results, 0, 0)
@@ -211,24 +245,27 @@
                 else:
                     ring[kind, s, lo : lo + n, cols(i)] = total.astype(BF16)
 
-        tiles(n_cols, body)
+        tiles(2, body)
         for s, step in ((0, -1), (1, 1)):
-            backs[kind, s, h] = send(
-                part(ring, kind, s, h), part(back, kind, s, h),
-                z_send.at[2 + kind, s, h - 1], z_recv.at[2 + kind, s, h - 1], at_z(step),
+            backs[kind, s, h, q] = send(
+                ring.at[kind, s, pl.ds(lo, n), chunk(q, 2)], back.at[kind, s, pl.ds(lo, n), chunk(q, 2)],
+                z_send.at[2 + kind, s, h - 1, q], z_recv.at[2 + kind, s, h - 1, q], at_z(step),
             )
 
-    def deliver(kind, target):
+    def deliver(kind, target, q):
         for s in range(2):
-            backs[kind, s, 1].wait_recv()
-
-        def body(i):
+            backs[kind, s, 1, q].wait_recv()
+
+        def body(k):
+            i = 2 * q + k
             total = dot(sel0[...], group(kind, 0, i), 0, 0)
             for s in range(2):
                 total = total + dot(place[s, :, : HOPS[0]], back[kind, s, : HOPS[0], cols(i)])
+            if kind == TOK:
+                total = weight * total
             target[:, cols(i)] = total.astype(BF16)
 
-        tiles(n_cols, body)
+        tiles(2, body)
 
     grads = (gdn, wg, wu)
     results = (gd_ref, gg_ref, gu_ref)
@@ -275,38 +312,48 @@
                 rs_send(m, stage, side, far + 2)
 
     def rs_finish(m, stage):
-        for upper, (a, b) in enumerate(((4, 2), (1, 5))):
-            for side in range(2):
-                _, p = place_of(stage, side)
+        for side in range(2):
+            _, p = place_of(stage, side)
+            totals = []
+            for upper, (a, b) in enumerate(((4, 2), (1, 5))):
                 where = view(m, stage, side, p, upper)
                 total = grads[m][where].astype(F32) + rs_got(m, stage, side, a) + rs_got(m, stage, side, b)
                 if stage == 0:
                     grads[m][where] = total.astype(BF16)
+                totals.append(total)
+            if stage == 1:
+                total = jnp.concatenate(totals, axis=0)
+                c = slice(side * half, (side + 1) * half)
+                if m == 0:
+                    gd_ref[c, :] = total.T
                 else:
-                    results[m][64 * upper : 64 * upper + 64, side * half : (side + 1) * half] = total
-
-    build(TOK, tok_ref)
+                    results[m][:, c] = total
+
+    build(TOK)
     pl.semaphore_wait(barrier, len(neighbours))
     forward_meta(1)
     forward(TOK, 1)
-    build(COT, cot_ref)
-    forward(COT, 1)
+    build(COT)
+    forward(COT, 1, 0, 4)
     for h in (1, 2, 3):
         choose(h)
         forward_meta(h + 1)
         arrived(TOK, h)
         forward(TOK, h + 1)
-        arrived(COT, h)
-        forward(COT, h + 1)
+        forward(COT, 1, h, 4)
         select(TOK, h)
-        select(COT, h)
+        swap_in(TOK, h)
     choose(4)
     arrived(TOK, 4)
     select(TOK, 4)
-    swap_in(TOK)
+    swap_in(TOK, 0)
     for load in loads:
         load.wait()
-    pairs[TOK].wait_recv()
+    swapped(TOK)
+    for q in range(4):
+        arrived(COT, 1, q)
+        if q % 2:
+            forward(COT, 2, q // 2, 2)
 
     def ff_tile(i):
         return pl.ds(pl.multiple_of(i * 256, 256), 256)
@@ -320,23 +367,40 @@
         hid[:, ff_tile(i)] = (gate * jax.nn.sigmoid(gate) * up).astype(BF16)
 
     tiles(ff // 256, up_body)
-
-    def down_body(i):
-        out[TOK, :, cols(i)] = dot(hid[...], wd[:, cols(i)]).astype(BF16)
-
-    tiles(n_cols, down_body)
-    swap_out(TOK)
-
-    arrived(COT, 4)
+    for i in range(n_cols):
+        c = slice(i * COLS, (i + 1) * COLS)
+        out[TOK, :, c] = dot(hid[...], wd[:, c]).astype(BF16)
+        swap_out(TOK, i)
+    select(COT, 1)
+    swap_in(COT, 1)
+    arrived(COT, 2, 0)
+    forward(COT, 3, 0, 2)
+
+    for s in range(2):
+        for h in (1, 2, 3, 4):
+            moves[TOK, s, h, 0].wait_send()
+    give_back(TOK, 4, 0)
+    arrived(COT, 2, 1)
+    forward(COT, 3, 1, 2)
+    give_back(TOK, 4, 1)
+    select(COT, 2)
+    swap_in(COT, 2)
+    arrived(COT, 3, 0)
+    forward(COT, 4, 0, 2)
+    arrived(COT, 3, 1)
+    forward(COT, 4, 1, 2)
+    give_back(TOK, 3, 0)
+    give_back(TOK, 3, 1)
+    select(COT, 3)
+    swap_in(COT, 3)
+    arrived(COT, 4, 0)
+    arrived(COT, 4, 1)
     select(COT, 4)
-    swap_in(COT)
-    for kind in (TOK, COT):
-        for h in (1, 2, 3, 4):
-            for s in range(2):
-                moves[kind, s, h].wait_send()
-    pairs[2 + TOK].wait_recv()
-    give_back(TOK, 4)
-    pairs[COT].wait_recv()
+    swap_in(COT, 0)
+    for s in range(2):
+        for h, q in ((1, 0), (1, 1), (1, 2), (1, 3), (2, 0), (2, 1), (3, 0), (3, 1), (4, 0), (4, 1)):
+            moves[COT, s, h, q].wait_send()
+    swapped(COT)
 
     def down_grad(i):
         gdn[i] = dot(work[COT, :, cols(i)], hid[...], 0, 0).astype(BF16).reshape(4, 128, ff)
@@ -344,7 +408,8 @@
     tiles(n_cols, down_grad)
     if with_dp:
         rs_start(0, 0)
-    give_back(TOK, 3)
+    give_back(TOK, 2, 0)
+    give_back(TOK, 2, 1)
 
     def grad_body(i):
         gh = dot(work[COT], wd[ff_tile(i), :], 1, 1)
@@ -354,14 +419,10 @@
         dgu[:, pl.ds(pl.multiple_of(ff + i * 256, 256), 256)] = (gh * (gate * s)).astype(BF16)
 
     tiles(ff // 256, grad_body)
-    give_back(TOK, 2)
-
-    def in_grad(i):
+    for i in range(n_cols):
         total = dot(dgu[:, :ff], wg[i].reshape(COLS, ff), 1, 1) + dot(dgu[:, ff:], wu[i].reshape(COLS, ff), 1, 1)
-        out[COT, :, cols(i)] = total.astype(BF16)
-
-    tiles(n_cols, in_grad)
-    swap_out(COT)
+        out[COT, :, i * COLS : (i + 1) * COLS] = total.astype(BF16)
+        swap_out(COT, i)
     if with_dp:
         rs_relay(0, 0)
 
@@ -373,38 +434,67 @@
     tiles(n_cols, up_grad)
     if with_dp:
         rs_start(1, 0)
-        rs_start(2, 0)
-    pairs[2 + COT].wait_recv()
-    give_back(COT, 4)
-    give_back(TOK, 1)
-    give_back(COT, 3)
+    give_back(COT, 4, 0)
+    give_back(COT, 4, 1)
+    give_back(TOK, 1, 0)
+    give_back(TOK, 1, 1)
     if with_dp:
         rs_finish(0, 0)
         rs_start(0, 1)
         rs_relay(1, 0)
-        rs_relay(2, 0)
+        rs_start(2, 0)
+    give_back(COT, 3, 0)
+    give_back(COT, 3, 1)
+    if with_dp:
         rs_relay(0, 1)
-    give_back(COT, 2)
-    if with_dp:
         rs_finish(1, 0)
         rs_start(1, 1)
-    give_back(COT, 1)
+        rs_relay(2, 0)
+    give_back(COT, 2, 0)
+    give_back(COT, 2, 1)
     if with_dp:
         rs_finish(0, 1)
+        rs_relay(1, 1)
+    deliver(TOK, comb_ref, 0)
+    deliver(TOK, comb_ref, 1)
+    give_back(COT, 1, 0)
+    give_back(COT, 1, 1)
+    if with_dp:
         rs_finish(2, 0)
         rs_start(2, 1)
-        rs_relay(1, 1)
+        rs_finish(1, 1)
         rs_relay(2, 1)
-    deliver(TOK, comb_ref)
-    if with_dp:
-        rs_finish(1, 1)
         rs_finish(2, 1)
     else:
         for ref in results:
             ref[...] = jnp.zeros_like(ref)
-    deliver(COT, gtok_ref)
+    deliver(COT, gtok_ref, 0)
+    deliver(COT, gtok_ref, 1)
     for copy in sends:
         copy.wait_send()
+
+
+def hand_over(*refs):
+    n = (len(refs) - 1) // 3
+    sources, targets, held, sems = refs[:n], refs[n : 2 * n], refs[2 * n : 3 * n], refs[-1]
+
+    def copies(a, b, step):
+        every = []
+        for i in range(n):
+            many = a[i].shape[0] // 2
+            for k in range(2):
+                piece = pl.ds(k * many, many)
+                every.append(pltpu.make_async_copy(a[i].at[piece], b[i].at[piece], sems.at[step, i, k]))
+        return every
+
+    loads, stores = copies(sources, held, 0), copies(held, targets, 1)
+    for load in loads:
+        load.start()
+    for load, store in zip(loads, stores):
+        load.wait()
+        store.start()
+    for store in stores:
+        store.wait()
 
 
 def local(tokens, expert_ids, gate_weights, w_gate, w_up, w_down, cotangent):
@@ -412,26 +502,26 @@
     ff = w_gate.shape[2]
     with_dp = lax.axis_size("dp") == 16
     shard = width // 16
-    weight = gate_weights[:, :1]
-    grad_out = (weight * cotangent.astype(F32)).astype(BF16)
     vmem, hbm = pl.BlockSpec(memory_space=pltpu.VMEM), pl.BlockSpec(memory_space=pl.ANY)
     dma = pltpu.SemaphoreType.DMA
-    combined, grad_tokens, grad_gate, grad_up, grad_down = pl.pallas_call(
+    shapes = (
+        jax.ShapeDtypeStruct((rows, width), BF16),
+        jax.ShapeDtypeStruct((rows, width), BF16),
+        jax.ShapeDtypeStruct((shard, ff), F32),
+        jax.ShapeDtypeStruct((shard, ff), F32),
+        jax.ShapeDtypeStruct((ff, shard), F32),
+    )
+    outs = pl.pallas_call(
         functools.partial(kernel, with_dp),
-        out_shape=(
-            jax.ShapeDtypeStruct((rows, width), BF16),
-            jax.ShapeDtypeStruct((rows, width), BF16),
-            jax.ShapeDtypeStruct((shard, ff), F32),
-            jax.ShapeDtypeStruct((shard, ff), F32),
-            jax.ShapeDtypeStruct((shard, ff), F32),
-        ),
-        in_specs=[vmem] * 5 + [hbm] * 3,
+        out_shape=shapes,
+        in_specs=[vmem] * 4 + [hbm] * 3,
         out_specs=(vmem,) * 5,
         scratch_shapes=[
             pltpu.VMEM((4, 4, shard, ff), BF16),
             pltpu.VMEM((4, 4, shard, ff), BF16),
             pltpu.VMEM((ff, width), BF16),
             pltpu.VMEM((4, 4, shard, ff), BF16),
+            pltpu.VMEM((rows, width), BF16),
             pltpu.VMEM((2, 2, HOPS[0], width), BF16),
             pltpu.VMEM((2, 2, ROWS, width), BF16),
             pltpu.VMEM((2, 2, ROWS, width), BF16),
@@ -449,12 +539,12 @@
             pltpu.VMEM((3, 2, 6, 2, shard, ff // 2), BF16),
             pltpu.VMEM((3, 2, 6, shard // 2, ff // 2), BF16),
             dma((3,)),
-            dma((4, 2, 4)),
-            dma((4, 2, 4)),
+            dma((4, 2, 4, 4)),
+            dma((4, 2, 4, 4)),
             dma((2, 4)),
             dma((2, 4)),
-            dma((4,)),
-            dma((4,)),
+            dma((4, 4)),
+            dma((4, 4)),
             dma((3, 2, 2, 6)),
             dma((3, 2, 2, 6)),
         ],
@@ -462,11 +552,17 @@
             collective_id=0, has_side_effects=True, vmem_limit_bytes=63 * 2**20
         ),
     )(
-        expert_ids, expert_ids.T, gate_weights, tokens, grad_out,
+        expert_ids.T, gate_weights.T, tokens, cotangent,
         w_gate.reshape(4, 4, shard, ff), w_up.reshape(4, 4, shard, ff), w_down.reshape(ff, width),
     )
-    combined = (weight * combined.astype(F32)).astype(BF16)
-    return (combined, grad_tokens, grad_gate[None], grad_up[None], grad_down.T[None])
+    combined, grad_tokens, grad_gate, grad_up, grad_down = pl.pallas_call(
+        hand_over,
+        out_shape=shapes,
+        in_specs=[hbm] * 5,
+        out_specs=(hbm,) * 5,
+        scratch_shapes=[pltpu.VMEM(s.shape, s.dtype) for s in shapes] + [dma((2, 5, 2))],
+    )(*outs)
+    return (combined, grad_tokens, grad_gate[None], grad_up[None], grad_down[None])
 
 
 def solution(mesh):

time: 173 us -> 142 us (0.82)
  Pallas kernels: 157 us -> 141 us
  local copies, waits for them, and re-layouts: 8.81 us -> 0 us
  other arithmetic: 4.04 us -> 0 us
    pallas_call x1 -> x2, Pallas kernels: 157 us -> 141 us  [the longest x1 138 us: local(): pl.pallas_call(functools.partial(kernel, with_dp), out_shape=shapes, in_s...]
    unnamed x10 -> x0, local copies, waits for them, and re-layouts: 8.12 us -> none
    convert_element_type x2 -> x0, other arithmetic: 4.04 us -> none  [the longest x1 2.06 us: local(): combined = (weight * combined.astype(F32)).astype(BF16)]
where the time goes in v3:
time: 142 us; the launch traced here: 141 us
  Pallas kernels  141 us (99%)
    pallas_call x1, Pallas kernels, local(): pl.pallas_call(functools.partial(kernel, with_dp), out_shape=shapes, in_s...  138 us

profile of v3, /device:TPU:1, one launch (start us, length us, event | category | flops | bytes accessed | tf_op | source)
XLA Modules:
  0.0 141.4 jit_solution(16770942089813471894)
XLA Ops:
  0.6 138.3 %shard_map.110 = (bf16[128,2048]{1,0:T(8,128)(2,1)}, bf16[128,2048]{1,0:T(8,128)(2,1)}, f32[128,768]{1,0:T(8,128)}, f32[128,768]{1,0:T(8,128)}, f32[768,128]{1,0:T(8,128)}) custom-call(s32[8,128]{1,0:T(8,128)} %bitcast.11, f32[8,128]{1,0:T(8,128)} %bitcast.12, bf16[128,2048]{1,0:T(8,128)(2,1)} %tok_ref.1, bf16[128,2048]{1,0:T(8,128)(2,1)} %cot_ref.1, ...), custom_call_target="tpu_custom_call" | custom-call | tf_op jit(solution)/shard_map/pallas_call | solution.py:514
  138.9 2.5 %shard_map.111 = (bf16[128,2048]{1,0:T(8,128)(2,1)}, bf16[128,2048]{1,0:T(8,128)(2,1)}, f32[128,768]{1,0:T(8,128)}, f32[128,768]{1,0:T(8,128)}, f32[768,128]{1,0:T(8,128)}) custom-call(bf16[128,2048]{1,0:T(8,128)(2,1)} %get-tuple-element.15.refs_0_, bf16[128,2048]{1,0:T(8,128)(2,1)} %get-tuple-element.16.refs_1_, f32[128,768]{1,0:T(8,128)} %get-tuple-element.17.refs_2_, ...), custom_call_target="tpu_custom_call" | custom-call | tf_op jit(solution)/shard_map/pallas_call | solution.py:558

commit v4 on v3

--- a/solution.py
+++ b/solution.py
@@ -24,9 +24,9 @@
 
 def kernel(
     with_dp, idst_ref, gwt_ref, tok_ref, cot_ref, wg_hbm, wu_hbm, wd_hbm,
-    comb_ref, gtok_ref, gg_ref, gu_ref, gd_ref,
-    wg, wu, wd, gdn, scaled, own, ring, back, meta, sel, sel0, place, work, away, out, near, pre, hid, dgu, rs0, rs1,
-    w_sem, z_send, z_recv, m_send, m_recv, p_send, p_recv, r_send, r_recv,
+    comb_hbm, gtok_hbm, gg_hbm, gu_hbm, gd_hbm, comb_ref, gtok_ref, gg_ref, gu_ref, gd_ref,
+    wg, wu, wd, gdn, ggt, gup, scaled, own, ring, back, meta, sel, sel0, place, work, away, out, near, pre, hid, dgu, x_t, hid_t, rs0, rs1, rs0d, rs1d,
+    w_sem, o_sem, z_send, z_recv, m_send, m_recv, p_send, p_recv, r_send, r_recv,
 ):
     rows, width = tok_ref.shape
     ff = hid.shape[1]
@@ -124,16 +124,15 @@
     def cols(i):
         return pl.ds(pl.multiple_of(i * COLS, COLS), COLS)
 
-    def build(kind):
-        def body(i):
-            if kind == TOK:
-                block = tok_ref[:, cols(i)]
-            else:
-                block = (weight * cot_ref[:, cols(i)].astype(F32)).astype(BF16)
-                scaled[:, cols(i)] = block
-            for s in range(2):
-                own[kind, s, :, cols(i)] = dot(place[s, :, : HOPS[0]], block, 0, 0).astype(BF16)
-        tiles(n_cols, body)
+    def build(kind, i):
+        c = slice(i * COLS, (i + 1) * COLS)
+        if kind == TOK:
+            block = tok_ref[:, c]
+        else:
+            block = (weight * cot_ref[:, c].astype(F32)).astype(BF16)
+            scaled[:, c] = block
+        for s in range(2):
+            own[kind, s, :, c] = dot(place[s], block, 0, 0).astype(BF16)
 
     sends = []
 
@@ -153,6 +152,13 @@
             metas[s, h] = send(
                 meta.at[s, h - 1], meta.at[s, h], m_send.at[s, h - 1], m_recv.at[s, h - 1], at_z(step)
             )
+
+    stores = []
+
+    def store(src, dst):
+        copy = pltpu.make_async_copy(src, dst, o_sem.at[len(stores)])
+        copy.start()
+        stores.append(copy)
 
     def chunk(q, n):
         return pl.ds(q * (width // n), width // n)
@@ -266,8 +272,9 @@
             target[:, cols(i)] = total.astype(BF16)
 
         tiles(2, body)
-
-    grads = (gdn, wg, wu)
+        store(target.at[:, chunk(q, 2)], (comb_hbm, gtok_hbm)[kind].at[:, chunk(q, 2)])
+
+    grads = (gdn, ggt, gup)
     results = (gd_ref, gg_ref, gu_ref)
     sums = {}
 
@@ -277,11 +284,20 @@
 
     def view(m, stage, side, dest, upper):
         c = slice(side * half, (side + 1) * half)
+        if m == 0:
+            if stage == 0:
+                many = slice(2 * upper, 2 * upper + 2)
+                return (many, dest, c) if side == 0 else (dest, many, c)
+            part = slice(side * half + upper * (half // 2), side * half + (upper + 1) * (half // 2))
+            return (dest, px, part) if side == 0 else (py, dest, part)
         if stage == 0:
             many = slice(2 * upper, 2 * upper + 2)
             return (many, dest, slice(None), c) if side == 0 else (dest, many, slice(None), c)
         many = slice(64 * upper, 64 * upper + 64)
         return (dest, px, many, c) if side == 0 else (py, dest, many, c)
+
+    def inbox(m, stage):
+        return ((rs0d, rs1d) if m == 0 else (rs0.at[m - 1], rs1.at[m - 1]))[stage]
 
     def rs_send(m, stage, side, slot):
         axis, p = place_of(stage, side)
@@ -290,16 +306,16 @@
         )[slot]
         where = view(m, stage, side, lax.rem(p + dest, 4), upper)
         sums[m, stage, side, slot] = send(
-            grads[m].at[where], (rs0, rs1)[stage].at[m, side, slot],
+            grads[m].at[where], inbox(m, stage).at[side, slot],
             r_send.at[m, stage, side, slot], r_recv.at[m, stage, side, slot], at_dp(axis, step),
         )
 
     def rs_got(m, stage, side, slot):
         sums[m, stage, side, slot].wait_recv()
-        return (rs0, rs1)[stage][m, side, slot].astype(F32)
-
-    def rs_start(m, stage):
-        for slot in (0, 3, 1, 4):
+        return inbox(m, stage)[side, slot].astype(F32)
+
+    def rs_start(m, stage, slots=(0, 3, 1, 4)):
+        for slot in slots:
             for side in range(2):
                 rs_send(m, stage, side, slot)
 
@@ -325,22 +341,33 @@
                 total = jnp.concatenate(totals, axis=0)
                 c = slice(side * half, (side + 1) * half)
                 if m == 0:
-                    gd_ref[c, :] = total.T
+                    gd_ref[c, :] = total
                 else:
                     results[m][:, c] = total
-
-    build(TOK)
+        if stage == 1:
+            store(results[m], (gd_hbm, gg_hbm, gu_hbm)[m])
+
+    build(TOK, 0)
     pl.semaphore_wait(barrier, len(neighbours))
     forward_meta(1)
-    forward(TOK, 1)
-    build(COT)
+    forward(TOK, 1, 0, 4)
+    for i in range(1, 4):
+        build(TOK, i)
+        forward(TOK, 1, i, 4)
+    for i in range(4):
+        build(COT, i)
     forward(COT, 1, 0, 4)
     for h in (1, 2, 3):
         choose(h)
         forward_meta(h + 1)
-        arrived(TOK, h)
+        for q in range(4 if h == 1 else 1):
+            arrived(TOK, h, q)
         forward(TOK, h + 1)
         forward(COT, 1, h, 4)
+        if h == 3:
+            arrived(COT, 1, 0)
+            arrived(COT, 1, 1)
+            forward(COT, 2, 0, 2)
         select(TOK, h)
         swap_in(TOK, h)
     choose(4)
@@ -349,11 +376,10 @@
     swap_in(TOK, 0)
     for load in loads:
         load.wait()
+    arrived(COT, 1, 2)
+    arrived(COT, 1, 3)
+    forward(COT, 2, 1, 2)
     swapped(TOK)
-    for q in range(4):
-        arrived(COT, 1, q)
-        if q % 2:
-            forward(COT, 2, q // 2, 2)
 
     def ff_tile(i):
         return pl.ds(pl.multiple_of(i * 256, 256), 256)
@@ -371,28 +397,33 @@
         c = slice(i * COLS, (i + 1) * COLS)
         out[TOK, :, c] = dot(hid[...], wd[:, c]).astype(BF16)
         swap_out(TOK, i)
+    arrived(COT, 2, 0)
+    forward(COT, 3, 0, 2)
     select(COT, 1)
     swap_in(COT, 1)
-    arrived(COT, 2, 0)
-    forward(COT, 3, 0, 2)
-
-    for s in range(2):
-        for h in (1, 2, 3, 4):
-            moves[TOK, s, h, 0].wait_send()
-    give_back(TOK, 4, 0)
     arrived(COT, 2, 1)
     forward(COT, 3, 1, 2)
-    give_back(TOK, 4, 1)
+
+    for s in range(2):
+        for h, q in ((1, 0), (1, 1), (1, 2), (1, 3), (2, 0), (3, 0), (4, 0)):
+            moves[TOK, s, h, q].wait_send()
+    give_back(TOK, 4, 0)
+    hid_t[...] = hid[...].T
+
+    def turn(i):
+        x_t[cols(i), :] = work[TOK, :, cols(i)].T
+
+    arrived(COT, 3, 0)
+    forward(COT, 4, 0, 2)
     select(COT, 2)
     swap_in(COT, 2)
-    arrived(COT, 3, 0)
-    forward(COT, 4, 0, 2)
     arrived(COT, 3, 1)
     forward(COT, 4, 1, 2)
-    give_back(TOK, 3, 0)
-    give_back(TOK, 3, 1)
+    give_back(TOK, 4, 1)
+    tiles(n_cols, turn)
     select(COT, 3)
     swap_in(COT, 3)
+    give_back(TOK, 3, 0)
     arrived(COT, 4, 0)
     arrived(COT, 4, 1)
     select(COT, 4)
@@ -400,16 +431,18 @@
     for s in range(2):
         for h, q in ((1, 0), (1, 1), (1, 2), (1, 3), (2, 0), (2, 1), (3, 0), (3, 1), (4, 0), (4, 1)):
             moves[COT, s, h, q].wait_send()
+    give_back(TOK, 3, 1)
     swapped(COT)
 
     def down_grad(i):
-        gdn[i] = dot(work[COT, :, cols(i)], hid[...], 0, 0).astype(BF16).reshape(4, 128, ff)
+        total = dot(hid_t[...], work[COT, :, cols(i)]).astype(BF16)
+        for k in range(4):
+            gdn[i, k] = total[:, 128 * k : 128 * k + 128]
 
     tiles(n_cols, down_grad)
     if with_dp:
         rs_start(0, 0)
     give_back(TOK, 2, 0)
-    give_back(TOK, 2, 1)
 
     def grad_body(i):
         gh = dot(work[COT], wd[ff_tile(i), :], 1, 1)
@@ -419,57 +452,64 @@
         dgu[:, pl.ds(pl.multiple_of(ff + i * 256, 256), 256)] = (gh * (gate * s)).astype(BF16)
 
     tiles(ff // 256, grad_body)
+    give_back(TOK, 2, 1)
+
+    def up_grad(i):
+        x = x_t[cols(i), :]
+        ggt[i] = dot(x, dgu[:, :ff]).astype(BF16).reshape(4, 128, ff)
+        gup[i] = dot(x, dgu[:, ff:]).astype(BF16).reshape(4, 128, ff)
+
+    tiles(n_cols, up_grad)
+    if with_dp:
+        rs_relay(0, 0)
+        rs_start(1, 0, (0, 3))
+        rs_start(2, 0, (0, 3))
+        rs_start(1, 0, (1, 4))
+        rs_start(2, 0, (1, 4))
+    give_back(TOK, 1, 0)
     for i in range(n_cols):
         total = dot(dgu[:, :ff], wg[i].reshape(COLS, ff), 1, 1) + dot(dgu[:, ff:], wu[i].reshape(COLS, ff), 1, 1)
         out[COT, :, i * COLS : (i + 1) * COLS] = total.astype(BF16)
         swap_out(COT, i)
     if with_dp:
-        rs_relay(0, 0)
-
-    def up_grad(i):
-        x = work[TOK, :, cols(i)]
-        wg[i] = dot(x, dgu[:, :ff], 0, 0).astype(BF16).reshape(4, 128, ff)
-        wu[i] = dot(x, dgu[:, ff:], 0, 0).astype(BF16).reshape(4, 128, ff)
-
-    tiles(n_cols, up_grad)
-    if with_dp:
-        rs_start(1, 0)
+        rs_finish(0, 0)
+        rs_start(0, 1)
     give_back(COT, 4, 0)
     give_back(COT, 4, 1)
-    give_back(TOK, 1, 0)
     give_back(TOK, 1, 1)
-    if with_dp:
-        rs_finish(0, 0)
-        rs_start(0, 1)
-        rs_relay(1, 0)
-        rs_start(2, 0)
     give_back(COT, 3, 0)
     give_back(COT, 3, 1)
     if with_dp:
-        rs_relay(0, 1)
-        rs_finish(1, 0)
-        rs_start(1, 1)
+        rs_relay(1, 0)
+    deliver(TOK, comb_ref, 0)
+    deliver(TOK, comb_ref, 1)
+    if with_dp:
         rs_relay(2, 0)
     give_back(COT, 2, 0)
     give_back(COT, 2, 1)
     if with_dp:
+        rs_relay(0, 1)
+    give_back(COT, 1, 0)
+    if with_dp:
+        rs_finish(1, 0)
+        rs_start(1, 1)
+    give_back(COT, 1, 1)
+    if with_dp:
         rs_finish(0, 1)
-        rs_relay(1, 1)
-    deliver(TOK, comb_ref, 0)
-    deliver(TOK, comb_ref, 1)
-    give_back(COT, 1, 0)
-    give_back(COT, 1, 1)
-    if with_dp:
         rs_finish(2, 0)
         rs_start(2, 1)
+        rs_relay(1, 1)
+        rs_relay(2, 1)
         rs_finish(1, 1)
-        rs_relay(2, 1)
         rs_finish(2, 1)
     else:
-        for ref in results:
+        for ref, target in zip(results, (gd_hbm, gg_hbm, gu_hbm)):
             ref[...] = jnp.zeros_like(ref)
+            store(ref, target)
     deliver(COT, gtok_ref, 0)
     deliver(COT, gtok_ref, 1)
+    for copy in stores:
+        copy.wait()
     for copy in sends:
         copy.wait_send()
 
@@ -515,11 +555,13 @@
         functools.partial(kernel, with_dp),
         out_shape=shapes,
         in_specs=[vmem] * 4 + [hbm] * 3,
-        out_specs=(vmem,) * 5,
-        scratch_shapes=[
+        out_specs=(hbm,) * 5,
+        scratch_shapes=[pltpu.VMEM(s.shape, s.dtype) for s in shapes] + [
             pltpu.VMEM((4, 4, shard, ff), BF16),
             pltpu.VMEM((4, 4, shard, ff), BF16),
             pltpu.VMEM((ff, width), BF16),
+            pltpu.VMEM((4, 4, ff, shard), BF16),
+            pltpu.VMEM((4, 4, shard, ff), BF16),
             pltpu.VMEM((4, 4, shard, ff), BF16),
             pltpu.VMEM((rows, width), BF16),
             pltpu.VMEM((2, 2, HOPS[0], width), BF16),
@@ -536,9 +578,14 @@
             pltpu.VMEM((2, 2 * PAIR, ff), F32),
             pltpu.VMEM((2 * PAIR, ff), BF16),
             pltpu.VMEM((2 * PAIR, 2 * ff), BF16),
-            pltpu.VMEM((3, 2, 6, 2, shard, ff // 2), BF16),
-            pltpu.VMEM((3, 2, 6, shard // 2, ff // 2), BF16),
+            pltpu.VMEM((width, 2 * PAIR), BF16),
+            pltpu.VMEM((ff, 2 * PAIR), BF16),
+            pltpu.VMEM((2, 2, 6, 2, shard, ff // 2), BF16),
+            pltpu.VMEM((2, 2, 6, shard // 2, ff // 2), BF16),
+            pltpu.VMEM((2, 6, 2, ff // 2, shard), BF16),
+            pltpu.VMEM((2, 6, ff // 4, shard), BF16),
             dma((3,)),
+            dma((7,)),
             dma((4, 2, 4, 4)),
             dma((4, 2, 4, 4)),
             dma((2, 4)),

time: 142 us -> 137 us (0.965)
  Pallas kernels: 141 us -> 136 us
    pallas_call x1, Pallas kernels: 138 us -> 133 us  [local(): pl.pallas_call(functools.partial(kernel, with_dp), out_shape=shapes, in_s...]
where the time goes in v4:
time: 137 us
  Pallas kernels  136 us (99%)
    pallas_call x1, Pallas kernels, local(): pl.pallas_call(functools.partial(kernel, with_dp), out_shape=shapes, in_s...  133 us

profile of v4, /device:TPU:1, one launch (start us, length us, event | category | flops | bytes accessed | tf_op | source)
XLA Modules:
  0.0 136.5 jit_solution(10936741241232610552)
XLA Ops:
  0.6 133.4 %shard_map.110 = (bf16[128,2048]{1,0:T(8,128)(2,1)}, bf16[128,2048]{1,0:T(8,128)(2,1)}, f32[128,768]{1,0:T(8,128)}, f32[128,768]{1,0:T(8,128)}, f32[768,128]{1,0:T(8,128)}) custom-call(s32[8,128]{1,0:T(8,128)} %bitcast.11, f32[8,128]{1,0:T(8,128)} %bitcast.12, bf16[128,2048]{1,0:T(8,128)(2,1)} %tok_ref.1, bf16[128,2048]{1,0:T(8,128)(2,1)} %cot_ref.1, ...), custom_call_target="tpu_custom_call" | custom-call | tf_op jit(solution)/shard_map/pallas_call | solution.py:554
  134.1 2.5 %shard_map.111 = (bf16[128,2048]{1,0:T(8,128)(2,1)}, bf16[128,2048]{1,0:T(8,128)(2,1)}, f32[128,768]{1,0:T(8,128)}, f32[128,768]{1,0:T(8,128)}, f32[768,128]{1,0:T(8,128)}) custom-call(bf16[128,2048]{1,0:T(8,128)(2,1)} %get-tuple-element.15.refs_0_, bf16[128,2048]{1,0:T(8,128)(2,1)} %get-tuple-element.16.refs_1_, f32[128,768]{1,0:T(8,128)} %get-tuple-element.17.refs_2_, ...), custom_call_target="tpu_custom_call" | custom-call | tf_op jit(solution)/shard_map/pallas_call | solution.py:605

commit v5 on v4

--- a/solution.py
+++ b/solution.py
@@ -23,12 +23,13 @@
 
 
 def kernel(
-    with_dp, idst_ref, gwt_ref, tok_ref, cot_ref, wg_hbm, wu_hbm, wd_hbm,
+    with_dp, idst_ref, gwt_ref, tok_hbm, cot_hbm, wg_hbm, wu_hbm, wd_hbm,
     comb_hbm, gtok_hbm, gg_hbm, gu_hbm, gd_hbm, comb_ref, gtok_ref, gg_ref, gu_ref, gd_ref,
+    tok_ref, cot_ref,
     wg, wu, wd, gdn, ggt, gup, scaled, own, ring, back, meta, sel, sel0, place, work, away, out, near, pre, hid, dgu, x_t, hid_t, rs0, rs1, rs0d, rs1d,
     w_sem, o_sem, z_send, z_recv, m_send, m_recv, p_send, p_recv, r_send, r_recv,
 ):
-    rows, width = tok_ref.shape
+    rows, width = tok_hbm.shape
     ff = hid.shape[1]
     half = ff // 2
     dp, ex = lax.axis_index("dp"), lax.axis_index("expert")
@@ -46,6 +47,17 @@
             return (py * 4 + lax.rem(px + step + 4, 4), ex)
         return (lax.rem(py + step + 4, 4) * 4 + px, ex)
 
+    load_tok = pltpu.make_async_copy(tok_hbm, tok_ref, w_sem.at[3])
+    load_cot = pltpu.make_async_copy(cot_hbm, cot_ref, w_sem.at[4])
+    load_tok.start()
+
+    neighbours = [at_z(1), at_z(-1), partner]
+    if with_dp:
+        neighbours += [at_dp(0, 1), at_dp(0, -1), at_dp(1, 1), at_dp(1, -1)]
+    barrier = pltpu.get_barrier_semaphore()
+    for device in neighbours:
+        pl.semaphore_signal(barrier, inc=1, device_id=device, device_id_type=MESH)
+    load_cot.start()
     loads = [
         pltpu.make_async_copy(wg_hbm, wg, w_sem.at[0]),
         pltpu.make_async_copy(wu_hbm, wu, w_sem.at[1]),
@@ -53,13 +65,6 @@
     ]
     for load in loads:
         load.start()
-
-    neighbours = [at_z(1), at_z(-1), partner]
-    if with_dp:
-        neighbours += [at_dp(0, 1), at_dp(0, -1), at_dp(1, 1), at_dp(1, -1)]
-    barrier = pltpu.get_barrier_semaphore()
-    for device in neighbours:
-        pl.semaphore_signal(barrier, inc=1, device_id=device, device_id_type=MESH)
 
     def distance(e):
         return ((e >> 1) - z) & 7
@@ -347,6 +352,7 @@
         if stage == 1:
             store(results[m], (gd_hbm, gg_hbm, gu_hbm)[m])
 
+    load_tok.wait()
     build(TOK, 0)
     pl.semaphore_wait(barrier, len(neighbours))
     forward_meta(1)
@@ -354,6 +360,7 @@
     for i in range(1, 4):
         build(TOK, i)
         forward(TOK, 1, i, 4)
+    load_cot.wait()
     for i in range(4):
         build(COT, i)
     forward(COT, 1, 0, 4)
@@ -481,32 +488,33 @@
     give_back(COT, 3, 1)
     if with_dp:
         rs_relay(1, 0)
+    give_back(COT, 2, 0)
+    if with_dp:
+        rs_relay(2, 0)
+    give_back(COT, 2, 1)
     deliver(TOK, comb_ref, 0)
     deliver(TOK, comb_ref, 1)
     if with_dp:
-        rs_relay(2, 0)
-    give_back(COT, 2, 0)
-    give_back(COT, 2, 1)
-    if with_dp:
         rs_relay(0, 1)
-    give_back(COT, 1, 0)
-    if with_dp:
         rs_finish(1, 0)
         rs_start(1, 1)
-    give_back(COT, 1, 1)
+    give_back(COT, 1, 0)
     if with_dp:
         rs_finish(0, 1)
         rs_finish(2, 0)
         rs_start(2, 1)
+    give_back(COT, 1, 1)
+    if with_dp:
         rs_relay(1, 1)
         rs_relay(2, 1)
         rs_finish(1, 1)
+    deliver(COT, gtok_ref, 0)
+    if with_dp:
         rs_finish(2, 1)
     else:
         for ref, target in zip(results, (gd_hbm, gg_hbm, gu_hbm)):
             ref[...] = jnp.zeros_like(ref)
             store(ref, target)
-    deliver(COT, gtok_ref, 0)
     deliver(COT, gtok_ref, 1)
     for copy in stores:
         copy.wait()
@@ -554,9 +562,11 @@
     outs = pl.pallas_call(
         functools.partial(kernel, with_dp),
         out_shape=shapes,
-        in_specs=[vmem] * 4 + [hbm] * 3,
+        in_specs=[vmem] * 2 + [hbm] * 5,
         out_specs=(hbm,) * 5,
         scratch_shapes=[pltpu.VMEM(s.shape, s.dtype) for s in shapes] + [
+            pltpu.VMEM((rows, width), BF16),
+            pltpu.VMEM((rows, width), BF16),
             pltpu.VMEM((4, 4, shard, ff), BF16),
             pltpu.VMEM((4, 4, shard, ff), BF16),
             pltpu.VMEM((ff, width), BF16),
@@ -584,7 +594,7 @@
             pltpu.VMEM((2, 2, 6, shard // 2, ff // 2), BF16),
             pltpu.VMEM((2, 6, 2, ff // 2, shard), BF16),
             pltpu.VMEM((2, 6, ff // 4, shard), BF16),
-            dma((3,)),
+            dma((5,)),
             dma((7,)),
             dma((4, 2, 4, 4)),
             dma((4, 2, 4, 4)),

time: 137 us -> 137 us (level)
  no operation moved by 1% of the time
where the time goes in v5:
time: 137 us
  Pallas kernels  136 us (99%)
    pallas_call x1, Pallas kernels, local(): pl.pallas_call(functools.partial(kernel, with_dp), out_shape=shapes, in_s...  133 us

profile of v5, /device:TPU:1, one launch (start us, length us, event | category | flops | bytes accessed | tf_op | source)
XLA Modules:
  0.0 136.5 jit_solution(14510120521636614295)
XLA Ops:
  0.6 133.4 %shard_map.110 = (bf16[128,2048]{1,0:T(8,128)(2,1)}, bf16[128,2048]{1,0:T(8,128)(2,1)}, f32[128,768]{1,0:T(8,128)}, f32[128,768]{1,0:T(8,128)}, f32[768,128]{1,0:T(8,128)}) custom-call(s32[8,128]{1,0:T(8,128)} %bitcast.11, f32[8,128]{1,0:T(8,128)} %bitcast.12, bf16[128,2048]{1,0:T(8,128)(2,1)} %tok_hbm.1, bf16[128,2048]{1,0:T(8,128)(2,1)} %cot_hbm.1, ...), custom_call_target="tpu_custom_call" | custom-call | tf_op jit(solution)/shard_map/pallas_call | solution.py:562
  134.0 2.5 %shard_map.111 = (bf16[128,2048]{1,0:T(8,128)(2,1)}, bf16[128,2048]{1,0:T(8,128)(2,1)}, f32[128,768]{1,0:T(8,128)}, f32[128,768]{1,0:T(8,128)}, f32[768,128]{1,0:T(8,128)}) custom-call(bf16[128,2048]{1,0:T(8,128)(2,1)} %get-tuple-element.15.refs_0_, bf16[128,2048]{1,0:T(8,128)(2,1)} %get-tuple-element.16.refs_1_, f32[128,768]{1,0:T(8,128)} %get-tuple-element.17.refs_2_, ...), custom_call_target="tpu_custom_call" | custom-call | tf_op jit(solution)/shard_map/pallas_call | solution.py:615

commit v6 on v5

--- a/solution.py
+++ b/solution.py
@@ -529,8 +529,8 @@
     def copies(a, b, step):
         every = []
         for i in range(n):
-            many = a[i].shape[0] // 2
-            for k in range(2):
+            many = a[i].shape[0] // 4
+            for k in range(4):
                 piece = pl.ds(k * many, many)
                 every.append(pltpu.make_async_copy(a[i].at[piece], b[i].at[piece], sems.at[step, i, k]))
         return every
@@ -617,7 +617,7 @@
         out_shape=shapes,
         in_specs=[hbm] * 5,
         out_specs=(hbm,) * 5,
-        scratch_shapes=[pltpu.VMEM(s.shape, s.dtype) for s in shapes] + [dma((2, 5, 2))],
+        scratch_shapes=[pltpu.VMEM(s.shape, s.dtype) for s in shapes] + [dma((2, 5, 4))],
     )(*outs)
     return (combined, grad_tokens, grad_gate[None], grad_up[None], grad_down[None])
 

time: 137 us -> 137 us (level)
  no operation moved by 1% of the time
where the time goes in v6:
time: 137 us
  Pallas kernels  136 us (99%)
    pallas_call x1, Pallas kernels, local(): pl.pallas_call(functools.partial(kernel, with_dp), out_shape=shapes, in_s...  133 us

profile of v6, /device:TPU:1, one launch (start us, length us, event | category | flops | bytes accessed | tf_op | source)
XLA Modules:
  0.0 136.7 jit_solution(11615408401401061270)
XLA Ops:
  0.6 133.4 %shard_map.110 = (bf16[128,2048]{1,0:T(8,128)(2,1)}, bf16[128,2048]{1,0:T(8,128)(2,1)}, f32[128,768]{1,0:T(8,128)}, f32[128,768]{1,0:T(8,128)}, f32[768,128]{1,0:T(8,128)}) custom-call(s32[8,128]{1,0:T(8,128)} %bitcast.11, f32[8,128]{1,0:T(8,128)} %bitcast.12, bf16[128,2048]{1,0:T(8,128)(2,1)} %tok_hbm.1, bf16[128,2048]{1,0:T(8,128)(2,1)} %cot_hbm.1, ...), custom_call_target="tpu_custom_call" | custom-call | tf_op jit(solution)/shard_map/pallas_call | solution.py:562
  134.0 2.7 %shard_map.111 = (bf16[128,2048]{1,0:T(8,128)(2,1)}, bf16[128,2048]{1,0:T(8,128)(2,1)}, f32[128,768]{1,0:T(8,128)}, f32[128,768]{1,0:T(8,128)}, f32[768,128]{1,0:T(8,128)}) custom-call(bf16[128,2048]{1,0:T(8,128)(2,1)} %get-tuple-element.15.refs_0_, bf16[128,2048]{1,0:T(8,128)(2,1)} %get-tuple-element.16.refs_1_, f32[128,768]{1,0:T(8,128)} %get-tuple-element.17.refs_2_, ...), custom_call_target="tpu_custom_call" | custom-call | tf_op jit(solution)/shard_map/pallas_call | solution.py:615
